TPU v7x, 32 devices: a whole 2x2x4 slice. The times are simulated.
32 devices in a mesh: fsdp: 8 (over z, core), ctx: 2 (over x), tp: 2 (over y).
Axes of the slice: x: 2, y: 2, z: 4, core: 2. Of those that a mesh axis runs over, the one named last changes fastest.
Arguments:
- tokens: bfloat16 [32, 1024, 768], P(('fsdp', 'tp'), 'ctx'), may hold values from -6 to 6
- query_key_value_weight: bfloat16 [768, 2304], P('fsdp'), may hold values from -0.21875 to 0.21875
- output_weight: bfloat16 [768, 768], P('fsdp'), may hold values from -3.5 to 3.5
- gate_weight: bfloat16 [768, 3072], P('fsdp', 'tp'), may hold values from -0.21875 to 0.21875
- up_weight: bfloat16 [768, 3072], P('fsdp', 'tp'), may hold values from -0.21875 to 0.21875
- down_weight: bfloat16 [3072, 768], P('tp', 'fsdp'), may hold values from -0.109375 to 0.109375
- gain_one: bfloat16 [768], P('fsdp'), may hold values from 0.25 to 1.75
- shift_one: bfloat16 [768], P('fsdp'), may hold values from -2.5 to 2.5
- gain_two: bfloat16 [768], P('fsdp'), may hold values from 0.25 to 1.75
- shift_two: bfloat16 [768], P('fsdp'), may hold values from -2.5 to 2.5
- lengths: int32 [32], P(('fsdp', 'tp')), may hold values from 256 to 1024, as said below
- positions: int32 [32, 1024], P(('fsdp', 'tp'), 'ctx'), may hold values from 0 to 2046, as said below
- cotangent: bfloat16 [32, 1024, 768], P(('fsdp', 'tp'), 'ctx'), may hold values from -6 to 6
Outputs:
- mixed_out: bfloat16 [32, 1024, 768], P(('fsdp', 'tp'), 'ctx')
- grad_tokens: float32 [32, 1024, 768], P(('fsdp', 'tp'), 'ctx')
- grad_w_qkv: float32 [768, 2304], P('fsdp')
- grad_w_out: float32 [768, 768], P('fsdp')
- grad_w_gate: float32 [768, 3072], P('fsdp', 'tp')
- grad_w_up: float32 [768, 3072], P('fsdp', 'tp')
- grad_w_down: float32 [3072, 768], P('tp', 'fsdp')
- grad_gain_one: float32 [768], P('fsdp')
- grad_shift_one: float32 [768], P('fsdp')
- grad_gain_two: float32 [768], P('fsdp')
- grad_shift_two: float32 [768], P('fsdp')
Inputs may be any that keep to these rules, and one draw needn't show every extreme that they name: `lengths`: each slot's valid tokens are its first ones; in each aligned block of 2 slots (the slots of one device) at least one slot holds 1024, which one drawn from the seed. `positions`: in each slot the first id is 0 and each next one is 1 or 2 larger; in some slot, drawn from the seed, every step is 2.
All inputs are finite; a program needn't handle non-finite values.
Results may differ from a plain program's by a relative error of at most 0.023.
Values may be sent and summed in bfloat16 or wider, within the bound.
No kernel may reach another device: no remote copies, remote signals or barrier semaphores. Data moves between devices by JAX's collectives and lax.ppermute only.
A program may use at most 192 MiB of HBM per device.

v0:
```python
import jax
import jax.numpy as jnp
from jax import lax
from jax.sharding import PartitionSpec as P

HEADS = 12
HEAD_DIM = 64


norm_eps = 1e-05
rope_base = 1000.0


def rotate(heads_in, places, direction):
    half_dim = heads_in.shape[-1] // 2
    frequency = rope_base ** (-jnp.arange(half_dim, dtype=jnp.float32) * 2.0 / heads_in.shape[-1])
    angles = places.astype(jnp.float32)[..., None] * frequency
    cosine = jnp.cos(angles)[..., None, :]
    sine_val = direction * jnp.sin(angles)[..., None, :]
    first_half = heads_in[..., :half_dim]
    second_half = heads_in[..., half_dim:]
    return jnp.concatenate(
        [
            first_half * cosine - second_half * sine_val,
            second_half * cosine + first_half * sine_val,
        ],
        axis=-1,
    )


def normalize(value_in, gain_in, shift_in):
    row_mean = jnp.mean(value_in, axis=-1, keepdims=True)
    centered = value_in - row_mean
    inverse = lax.rsqrt(jnp.mean(centered * centered, axis=-1, keepdims=True) + norm_eps)
    normed = centered * inverse
    return (normed * gain_in + shift_in, normed, inverse)


def normalize_back(normed, inverse, gain_in, upstream):
    scaled = upstream * gain_in
    grad_in = inverse * (
        scaled
        - jnp.mean(scaled, axis=-1, keepdims=True)
        - normed * jnp.mean(scaled * normed, axis=-1, keepdims=True)
    )
    return (grad_in, jnp.sum(upstream * normed, axis=(0, 1)), jnp.sum(upstream, axis=(0, 1)))


def masked_scores(queries, key_rows, length):
    score_scale = queries.shape[-1] ** (-0.5)
    scores = (
        jnp.einsum("qhe,khe->hqk", queries, key_rows, preferred_element_type=jnp.float32)
        * score_scale
    )
    valid_keys = jnp.arange(key_rows.shape[0]) < length
    return jnp.where(valid_keys, scores, -1000000000.0)


def block_forward(queries, key_rows, values, length):
    scores = masked_scores(queries, key_rows, length)
    row_top = jnp.max(scores, axis=-1, keepdims=True)
    exponent = jnp.exp(scores - row_top)
    row_total = jnp.sum(exponent, axis=-1, keepdims=True)
    softmax_out = (exponent / row_total).astype(jnp.bfloat16)
    context_value = jnp.einsum(
        "hqk,khe->qhe", softmax_out, values, preferred_element_type=jnp.float32
    )
    return (context_value, (row_top + jnp.log(row_total))[..., 0])


def block_backward(queries, key_rows, values, length, summit, grad_context):
    score_scale = queries.shape[-1] ** (-0.5)
    scores = masked_scores(queries, key_rows, length)
    softmax_out = jnp.exp(scores - summit[..., None])
    grad_probs = jnp.einsum(
        "qhe,khe->hqk", grad_context, values, preferred_element_type=jnp.float32
    )
    row_dot = jnp.sum(grad_probs * softmax_out, axis=-1, keepdims=True)
    grad_scores = (softmax_out * (grad_probs - row_dot)).astype(jnp.bfloat16)
    grad_query = (
        jnp.einsum("hqk,khe->qhe", grad_scores, key_rows, preferred_element_type=jnp.float32)
        * score_scale
    )
    grad_keys = (
        jnp.einsum("hqk,qhe->khe", grad_scores, queries, preferred_element_type=jnp.float32)
        * score_scale
    )
    grad_values = jnp.einsum(
        "hqk,qhe->khe",
        softmax_out.astype(jnp.bfloat16),
        grad_context,
        preferred_element_type=jnp.float32,
    )
    return (grad_query, grad_keys, grad_values)


def split_heads(heads_all):
    slot_count, seq_len, three, features = heads_all.shape
    local_heads = features // HEAD_DIM
    shaped = heads_all.reshape(slot_count, seq_len, 3, local_heads, HEAD_DIM)
    return (shaped[:, :, 0], shaped[:, :, 1], shaped[:, :, 2])


def query_blocks(array_in):
    slot_count, seq_len = (array_in.shape[0], array_in.shape[1])
    block_rows = min(512, seq_len)
    shaped = array_in.reshape((slot_count, seq_len // block_rows, block_rows) + array_in.shape[2:])
    return jnp.swapaxes(shaped, 0, 1)


def attention(heads_all, lengths):
    queries, key_rows, values = split_heads(heads_all)
    slot_count, seq_len, local_heads = (queries.shape[0], queries.shape[1], queries.shape[2])

    def run_block(query_part):
        return jax.vmap(block_forward)(query_part, key_rows, values, lengths)

    context_value, summit = lax.map(run_block, query_blocks(queries))
    context_value = jnp.swapaxes(context_value, 0, 1).reshape(
        slot_count, seq_len, local_heads * HEAD_DIM
    )
    return (context_value, summit)


def attention_back(heads_all, lengths, summit, grad_heads):
    queries, key_rows, values = split_heads(heads_all)
    slot_count, seq_len, local_heads = (queries.shape[0], queries.shape[1], queries.shape[2])
    grad_shaped = grad_heads.reshape(slot_count, seq_len, local_heads, HEAD_DIM)

    def run_block(carried, pieces):
        query_part, summit_part, grad_part = pieces
        grad_query, grad_keys, grad_values = jax.vmap(block_backward)(
            query_part, key_rows, values, lengths, summit_part, grad_part
        )
        return ((carried[0] + grad_keys, carried[1] + grad_values), grad_query)

    zeros_init = jnp.zeros(key_rows.shape, jnp.float32)
    (grad_keys, grad_values), grad_query = lax.scan(
        run_block,
        (zeros_init, zeros_init),
        (query_blocks(queries), summit, query_blocks(grad_shaped)),
    )
    grad_query = jnp.swapaxes(grad_query, 0, 1).reshape(slot_count, seq_len, local_heads, HEAD_DIM)
    stacked = jnp.stack([grad_query, grad_keys, grad_values], axis=2)
    return stacked.reshape(slot_count, seq_len, 3, local_heads * HEAD_DIM)


def shard_attention(gradients):
    return (
        lax.psum_scatter(
            gradients[0].astype(jnp.bfloat16), "fsdp", scatter_dimension=0, tiled=True
        ).astype(jnp.float32),
        lax.psum_scatter(
            gradients[1].astype(jnp.bfloat16), "fsdp", scatter_dimension=0, tiled=True
        ).astype(jnp.float32),
        lax.psum_scatter(
            gradients[2].astype(jnp.bfloat16), "fsdp", scatter_dimension=0, tiled=True
        ).astype(jnp.float32),
        lax.psum_scatter(
            gradients[3].astype(jnp.bfloat16), "fsdp", scatter_dimension=0, tiled=True
        ).astype(jnp.float32),
        lax.psum_scatter(
            gradients[4].astype(jnp.bfloat16), "fsdp", scatter_dimension=0, tiled=True
        ).astype(jnp.float32),
        lax.psum_scatter(
            gradients[5].astype(jnp.bfloat16), "fsdp", scatter_dimension=0, tiled=True
        ).astype(jnp.float32),
    )


def join_attention(gradients):
    return (
        lax.psum(gradients[0].astype(jnp.bfloat16), ("ctx", "tp")).astype(jnp.float32),
        lax.psum(gradients[1].astype(jnp.bfloat16), ("ctx", "tp")).astype(jnp.float32),
        lax.psum(gradients[2].astype(jnp.bfloat16), ("ctx", "tp")).astype(jnp.float32),
        lax.psum(gradients[3].astype(jnp.bfloat16), ("ctx", "tp")).astype(jnp.float32),
        lax.psum(gradients[4].astype(jnp.bfloat16), ("ctx", "tp")).astype(jnp.float32),
        lax.psum(gradients[5].astype(jnp.bfloat16), ("ctx", "tp")).astype(jnp.float32),
    )


def shard_feed(gradients):
    return (
        lax.psum_scatter(
            gradients[0].astype(jnp.bfloat16), "fsdp", scatter_dimension=0, tiled=True
        ).astype(jnp.float32),
        lax.psum_scatter(
            gradients[1].astype(jnp.bfloat16), "fsdp", scatter_dimension=0, tiled=True
        ).astype(jnp.float32),
        lax.psum_scatter(
            gradients[2].astype(jnp.bfloat16), "fsdp", scatter_dimension=1, tiled=True
        ).astype(jnp.float32),
    )


def join_feed(gradients):
    return (
        lax.psum(gradients[0].astype(jnp.bfloat16), "ctx").astype(jnp.float32),
        lax.psum(gradients[1].astype(jnp.bfloat16), "ctx").astype(jnp.float32),
        lax.psum(gradients[2].astype(jnp.bfloat16), "ctx").astype(jnp.float32),
    )


def on_device(
    tokens,
    query_key_value_weight,
    output_weight,
    gate_weight,
    up_weight,
    down_weight,
    gain_one,
    shift_one,
    gain_two,
    shift_two,
    lengths,
    positions,
    cotangent,
):
    (
        projection_complete,
        output_complete,
        gate_complete,
        up_complete,
        down_complete,
        gain_a,
        shift_a,
        gain_b,
        shift_b,
    ) = (
        lax.all_gather(query_key_value_weight, "fsdp", axis=0, tiled=True),
        lax.all_gather(output_weight, "fsdp", axis=0, tiled=True),
        lax.all_gather(gate_weight, "fsdp", axis=0, tiled=True),
        lax.all_gather(up_weight, "fsdp", axis=0, tiled=True),
        lax.all_gather(down_weight, "fsdp", axis=1, tiled=True),
        lax.all_gather(gain_one, "fsdp", axis=0, tiled=True),
        lax.all_gather(shift_one, "fsdp", axis=0, tiled=True),
        lax.all_gather(gain_two, "fsdp", axis=0, tiled=True),
        lax.all_gather(shift_two, "fsdp", axis=0, tiled=True),
    )
    gain_a = gain_a.astype(jnp.float32)
    shift_a = shift_a.astype(jnp.float32)
    gain_b = gain_b.astype(jnp.float32)
    shift_b = shift_b.astype(jnp.float32)
    slot_count, row_count, model_width = tokens.shape
    unrotated_projection = jnp.einsum(
        "gfi,in->gfn", tokens, projection_complete, preferred_element_type=jnp.float32
    )
    unrotated_projection = unrotated_projection.reshape(slot_count, row_count, 3, HEADS, HEAD_DIM)
    turned_query = rotate(unrotated_projection[:, :, 0], positions, 1.0)
    turned_keys = rotate(unrotated_projection[:, :, 1], positions, 1.0)
    packed = jnp.stack([turned_query, turned_keys, unrotated_projection[:, :, 2]], axis=2)
    packed = packed.reshape(slot_count, row_count, 3, model_width).astype(jnp.bfloat16)
    heads_all = lax.all_to_all(packed, "ctx", split_axis=3, concat_axis=1, tiled=True)
    context_value, summit = attention(heads_all, lengths)
    context_matrix = lax.all_to_all(
        context_value.astype(jnp.bfloat16), "ctx", split_axis=1, concat_axis=2, tiled=True
    )
    attention_result = jnp.einsum(
        "gfi,in->gfn", context_matrix, output_complete, preferred_element_type=jnp.float32
    )
    normed_one_out, normed_one, inverse_one = normalize(
        tokens.astype(jnp.float32) + attention_result, gain_a, shift_a
    )
    feed_input = lax.all_gather(normed_one_out.astype(jnp.bfloat16), "tp", axis=0, tiled=True)
    gate_preactivation = jnp.einsum(
        "zmc,ci->zmi", feed_input, gate_complete, preferred_element_type=jnp.float32
    )
    upper_output = jnp.einsum(
        "zmc,ci->zmi", feed_input, up_complete, preferred_element_type=jnp.float32
    )
    sigmoid_gate = jax.nn.sigmoid(gate_preactivation)
    hidden_state = (gate_preactivation * sigmoid_gate * upper_output).astype(jnp.bfloat16)
    partial_result = jnp.einsum(
        "pin,nw->piw", hidden_state, down_complete, preferred_element_type=jnp.float32
    )
    branch_output = lax.psum_scatter(partial_result, "tp", scatter_dimension=0, tiled=True)
    result, normed_two, inverse_two = normalize(normed_one_out + branch_output, gain_b, shift_b)
    grad_mix_two, grad_gain_b, grad_shift_b = normalize_back(
        normed_two, inverse_two, gain_b, cotangent.astype(jnp.float32)
    )
    gradient_total = lax.all_gather(grad_mix_two.astype(jnp.bfloat16), "tp", axis=0, tiled=True)
    down_gradient = jnp.einsum(
        "uqg,uqk->gk", hidden_state, gradient_total, preferred_element_type=jnp.float32
    )
    hidden_gradient = jnp.einsum(
        "ecq,jq->ecj", gradient_total, down_complete, preferred_element_type=jnp.float32
    )
    gate_gradient = (
        hidden_gradient
        * upper_output
        * sigmoid_gate
        * (1.0 + gate_preactivation * (1.0 - sigmoid_gate))
    ).astype(jnp.bfloat16)
    upper_gradient = (hidden_gradient * gate_preactivation * sigmoid_gate).astype(jnp.bfloat16)
    gate_weight_gradient = jnp.einsum(
        "vaq,vaz->qz", feed_input, gate_gradient, preferred_element_type=jnp.float32
    )
    up_weight_gradient = jnp.einsum(
        "vaq,vaz->qz", feed_input, upper_gradient, preferred_element_type=jnp.float32
    )
    feed_partial = jnp.einsum(
        "eyk,qk->eyq", gate_gradient, gate_complete, preferred_element_type=jnp.float32
    )
    feed_partial = feed_partial + jnp.einsum(
        "eyk,qk->eyq", upper_gradient, up_complete, preferred_element_type=jnp.float32
    )
    grad_feed = lax.psum_scatter(feed_partial, "tp", scatter_dimension=0, tiled=True)
    grad_mix_one, grad_gain_a, grad_shift_a = normalize_back(
        normed_one, inverse_one, gain_a, grad_mix_two + grad_feed
    )
    attention_gradient = grad_mix_one.astype(jnp.bfloat16)
    grad_out_w = jnp.einsum(
        "kpw,kpa->wa", context_matrix, attention_gradient, preferred_element_type=jnp.float32
    )
    grad_context = jnp.einsum(
        "cuw,yw->cuy", attention_gradient, output_complete, preferred_element_type=jnp.float32
    ).astype(jnp.bfloat16)
    grad_heads = lax.all_to_all(grad_context, "ctx", split_axis=2, concat_axis=1, tiled=True)
    grad_qkv_heads = attention_back(heads_all, lengths, summit, grad_heads)
    grad_qkv_rows = lax.all_to_all(
        grad_qkv_heads.astype(jnp.bfloat16), "ctx", split_axis=1, concat_axis=3, tiled=True
    ).astype(grad_qkv_heads.dtype)
    grad_split = grad_qkv_rows.reshape(slot_count, row_count, 3, HEADS, HEAD_DIM)
    back_query = rotate(grad_split[:, :, 0], positions, -1.0)
    back_keys = rotate(grad_split[:, :, 1], positions, -1.0)
    unrotated_gradient = jnp.stack([back_query, back_keys, grad_split[:, :, 2]], axis=2)
    unrotated_gradient = unrotated_gradient.reshape(slot_count, row_count, 3 * model_width).astype(
        jnp.bfloat16
    )
    projection_weight_gradient = jnp.einsum(
        "kpw,kpa->wa", tokens, unrotated_gradient, preferred_element_type=jnp.float32
    )
    grad_inputs = grad_mix_one + jnp.einsum(
        "cuw,yw->cuy", unrotated_gradient, projection_complete, preferred_element_type=jnp.float32
    )
    attention_grads = (
        projection_weight_gradient,
        grad_out_w,
        grad_gain_a,
        grad_shift_a,
        grad_gain_b,
        grad_shift_b,
    )
    feed_grads = (gate_weight_gradient, up_weight_gradient, down_gradient)
    attention_grads = shard_attention(join_attention(attention_grads))
    feed_grads = shard_feed(join_feed(feed_grads))
    return (
        result.astype(jnp.bfloat16),
        grad_inputs,
        attention_grads[0],
        attention_grads[1],
        feed_grads[0],
        feed_grads[1],
        feed_grads[2],
        attention_grads[2],
        attention_grads[3],
        attention_grads[4],
        attention_grads[5],
    )


def solution(mesh):
    in_specs = (
        P(("fsdp", "tp"), "ctx", None),
        P("fsdp", None),
        P("fsdp", None),
        P("fsdp", "tp"),
        P("fsdp", "tp"),
        P("tp", "fsdp"),
        P("fsdp"),
        P("fsdp"),
        P("fsdp"),
        P("fsdp"),
        P(("fsdp", "tp")),
        P(("fsdp", "tp"), "ctx"),
        P(("fsdp", "tp"), "ctx", None),
    )
    out_specs = (
        P(("fsdp", "tp"), "ctx", None),
        P(("fsdp", "tp"), "ctx", None),
        P("fsdp", None),
        P("fsdp", None),
        P("fsdp", "tp"),
        P("fsdp", "tp"),
        P("tp", "fsdp"),
        P("fsdp"),
        P("fsdp"),
        P("fsdp"),
        P("fsdp"),
    )
    return jax.shard_map(
        on_device, mesh=mesh, in_specs=in_specs, out_specs=out_specs, check_vma=False
    )
```

profile of v0, /device:TPU:0, one launch (start us, length us, event | category | flops | bytes accessed | tf_op | source)
XLA Modules:
  0.0 1124.1 jit_solution(9072271324689938630)
XLA Ops:
  9.8 44.1 %all-gather.8.cloned.1.call-done = bf16[768,2304]{1,0:T(8,128)(2,1)} async-done(((bf16[96,2304]{1,0:T(8,128)(2,1)}), bf16[768,2304]{1,0:T(8,128)(2,1)}) %all-gather.8.cloned.1.call-update) | async-done | bytes 3538960 | tf_op jit(solution)/shard_map/all_gather | solution.py:230
  82.7 52.2 %all-to-all-done = bf16[2,512,3,768]{1,0,2,3:T(2,128)(2,1)} async-done(((bf16[2,512,3,768]{1,0,2,3:T(2,128)(2,1)}), bf16[2,512,3,768]{1,0,2,3:T(2,128)(2,1)}, u32[]{:S(2)}, u32[]{:S(2)}) %all-to-all-start) | async-done | bytes 4718624 | tf_op jit(solution)/shard_map/all_to_all | solution.py:253
  168.3 68.0 %while.27 = (s32[]{:T(128)}, bf16[2,2,512,6,64]{2,4,3,1,0:T(8,128)(2,1)}, f32[2,2,6,512]{3,2,1,0:T(8,128)S(1)}, s32[2]{0:T(128)S(1)}, bf16[2,2,512,6,64]{2,4,3,1...) while((s32[]{:T(128)}, ...), condition=%wide.region_3.4_spmd, body=%wide.region_0.3_spmd.sunk | while | flops 1686106112 | bytes 100126920 | solution.py:118
  255.9 14.4 %all-reduce.9 = (bf16[768]{0:T(1024)(128)(2,1)S(1)}, bf16[768]{0:T(1024)(128)(2,1)S(1)}, bf16[768]{0:T(1024)(128)(2,1)S(1)}) all-reduce(bf16[768]{0:T(1024)(128)(2,1)S(1)} %dynamic-update-slice.1, bf16[768]{0:T(1024)(128)(2,1)S(1)} %dynamic-update-slice, ...), channel_id=1, replica_groups=mesh['fsdp'=8,'ctx'=2,'tp'=2] {'fsdp'}, use_global_device_ids=true, to_apply=%add.1 | all-reduce | flops 2304 | bytes 9216
  284.4 41.8 %all-gather.12.cloned.1.call-done = bf16[4,512,768]{2,1,0:T(8,128)(2,1)} async-done(((bf16[2,512,768]{2,1,0:T(8,128)(2,1)}), bf16[4,512,768]{2,1,0:T(8,128)(2,1)}) %all-gather.12.cloned.1.call-update) | async-done | bytes 3145744 | tf_op jit(solution)/shard_map/all_gather | solution.py:264
  336.2 23.1 %all-gather.16.cloned.1.call-done = bf16[768,1536]{1,0:T(8,128)(2,1)} async-done(((bf16[96,1536]{1,0:T(8,128)(2,1)}), bf16[768,1536]{1,0:T(8,128)(2,1)}) %all-gather.16.cloned.1.call-update) | async-done | bytes 2359312 | tf_op jit(solution)/shard_map/all_gather | solution.py:233
  359.4 14.2 %multiply_convert_fusion.3 = (bf16[4,512,1536]{2,1,0:T(8,128)(2,1)}, f32[4,512,1536]{2,1,0:T(8,128)}) fusion(f32[4,512,1536]{2,1,0:T(8,128)} %fusion.55, bf16[4,512,768]{2,1,0:T(8,128)(2,1)} %all-gather.12.cloned.1.call-done, bf16[768,1536]{1,0:T(8,128)(2,1)} %all-gather.16.cloned.1.call-done), kind=kOutput, calls=%fused_computation.44 | convolution fusion | flops 4850712576 | bytes 36962304 | tf_op jit(solution)/shard_map/zmc,ci->zmi/dot_general | solution.py:268
  373.6 18.0 %all-gather.18.cloned.1.call-done = bf16[1536,768]{0,1:T(8,128)(2,1)} async-done(((bf16[1536,96]{0,1:T(8,128)(2,1)}), bf16[1536,768]{0,1:T(8,128)(2,1)}) %all-gather.18.cloned.1.call-update) | async-done | bytes 2359312 | tf_op jit(solution)/shard_map/all_gather | solution.py:234
  401.3 76.3 %reduce-scatter.10.cloned.1.call-done = f32[2,512,768]{2,1,0:T(8,128)} async-done(((f32[4,512,768]{2,1,0:T(8,128)}), f32[2,512,768]{2,1,0:T(8,128)}) %reduce-scatter.10.cloned.1.call-update) | async-done | bytes 3145744 | tf_op jit(solution)/shard_map/reduce_scatter | solution.py:276
  488.1 45.0 %all-gather.20.cloned.1.call-done = bf16[4,512,768]{2,1,0:T(8,128)(2,1)} async-done(((bf16[2,512,768]{2,1,0:T(8,128)(2,1)}), bf16[4,512,768]{2,1,0:T(8,128)(2,1)}) %all-gather.20.cloned.1.call-update) | async-done | bytes 3145744 | tf_op jit(solution)/shard_map/all_gather | solution.py:281
  533.2 19.1 %multiply_convert_fusion.2 = (bf16[4,512,1536]{2,1,0:T(8,128)(2,1)}, bf16[4,512,1536]{2,1,0:T(8,128)(2,1)}) fusion(f32[4,512,1536]{2,1,0:T(8,128)} %fusion.55, f32[4,512,1536]{2,1,0:T(8,128)} %get-tuple-element.290, bf16[4,512,768]{2,1,0:T(8,128)(2,1)} %all-gather.20.cloned.1.call-done, bf16[1536,768]{0,1:T(8,128)(2,1)} %all-gather.18.cloned.1.call-done), kind=kOutput, calls=%fused_computation.43 | convolution fusion | flops 4872732672 | bytes 43253760 | tf_op jit(solution)/shard_map/ecq,jq->ecj/dot_general | solution.py:285
  586.1 57.7 %reduce-scatter.12.cloned.1.call-done = f32[2,512,768]{2,1,0:T(8,128)} async-done(((f32[4,512,768]{2,1,0:T(8,128)}), f32[2,512,768]{2,1,0:T(8,128)}) %reduce-scatter.12.cloned.1.call-update) | async-done | bytes 3145744 | tf_op jit(solution)/shard_map/reduce_scatter | solution.py:307
  688.6 163.5 %while.28 = (s32[]{:T(128)}, f32[2,1024,6,64]{1,3,2,0:T(8,128)}, f32[2,1024,6,64]{1,3,2,0:T(8,128)}, bf16[2,2,512,6,64]{2,4,3,1,0:T(8,128)(2,1)}, bf16[2,2,512,6...) while((s32[]{:T(128)}, f32[2,1024,6,64]{1,3,2,0:T(8,128)}, ...), condition=%wide.region_16.17_spmd.clone, body=%wide.region_14.16_spmd.clone.sunk | while | flops 4125224960 | bytes 217245872 | solution.py:138
  699.2 13.1 %bitcast_add_fusion.5 = f32[2,1024,6,64]{1,3,2,0:T(8,128)} fusion(f32[2,1024,6,64]{1,3,2,0:T(8,128)} %get-tuple-element.443, f32[2,6,512,1024]{3,2,1,0:T(8,128)} %fusion.128, f32[2,6,512]{2,1,0:T(8,128)S(1)} %dynamic-slice_bitcast_fusion.2, pred[2,1024]{1,0:T(4,128)(4,1)S(1)} %iota_compare_fusion.5, pred[]{:T(512)S(6)} %compare.3, ...), kind=kOutput, calls=%fused_computation.21.clone.1 | convolution fusion | flops 832045056 | bytes 32280580 | tf_op jit(solution)/shard_map/while/body/eval_jaxpr/vmap(hqk,qhe->khe)/dot_general | solution.py:88
  712.3 17.7 %multiply_reduce_fusion.7 = (f32[2,6,512]{2,1,0:T(8,128)S(1)}, f32[2,6,512,1024]{3,2,1,0:T(8,128)}) fusion(f32[2,6,512,1024]{3,2,1,0:T(8,128)} %fusion.128, f32[2,6,512]{2,1,0:T(8,128)S(1)} %dynamic-slice_bitcast_fusion.2, pred[2,1024]{1,0:T(4,128)(4,1)S(1)} %iota_compare_fusion.5, bf16[2,1024,6,64]{1,3,2,0:T(8,128)(2,1)} %get-tuple-element.462, ...), kind=kOutput, calls=%fused_computation.16.clone.1 | convolution fusion | flops 836757504 | bytes 52742148 | tf_op jit(solution)/shard_map/while/body/eval_jaxpr/vmap(qhe,khe->hqk)/dot_general | solution.py:75
  730.0 22.0 %multiply_convert_fusion.5 = bf16[2,6,512,1024]{3,2,1,0:T(8,128)(2,1)} fusion(f32[2,6,512,1024]{3,2,1,0:T(8,128)} %get-tuple-element.403, f32[2,6,512,1024]{3,2,1,0:T(8,128)} %fusion.128, f32[2,6,512]{2,1,0:T(8,128)S(1)} %get-tuple-element.404, f32[2,6,512]{2,1,0:T(8,128)S(1)} %dynamic-slice_bitcast_fusion.2, pred[2,1024]{1,0:T(4,128)(4,1)S(1)} %iota_compare_fusion.5), kind=kLoop, calls=%fused_computation.15.clone.1 | loop fusion | flops 37748736 | bytes 62965760 | tf_op jit(solution)/shard_map/while/body/eval_jaxpr/vmap()/convert_element_type | solution.py:79
  780.3 13.8 %bitcast_add_fusion.5 = f32[2,1024,6,64]{1,3,2,0:T(8,128)} fusion(f32[2,1024,6,64]{1,3,2,0:T(8,128)} %get-tuple-element.443, f32[2,6,512,1024]{3,2,1,0:T(8,128)} %fusion.128, f32[2,6,512]{2,1,0:T(8,128)S(1)} %dynamic-slice_bitcast_fusion.2, pred[2,1024]{1,0:T(4,128)(4,1)S(1)} %iota_compare_fusion.5, pred[]{:T(512)S(6)} %compare.3, ...), kind=kOutput, calls=%fused_computation.21.clone.1 | convolution fusion | flops 832045056 | bytes 32280580 | tf_op jit(solution)/shard_map/while/body/eval_jaxpr/vmap(hqk,qhe->khe)/dot_general | solution.py:88
  794.1 17.4 %multiply_reduce_fusion.7 = (f32[2,6,512]{2,1,0:T(8,128)S(1)}, f32[2,6,512,1024]{3,2,1,0:T(8,128)}) fusion(f32[2,6,512,1024]{3,2,1,0:T(8,128)} %fusion.128, f32[2,6,512]{2,1,0:T(8,128)S(1)} %dynamic-slice_bitcast_fusion.2, pred[2,1024]{1,0:T(4,128)(4,1)S(1)} %iota_compare_fusion.5, bf16[2,1024,6,64]{1,3,2,0:T(8,128)(2,1)} %get-tuple-element.462, ...), kind=kOutput, calls=%fused_computation.16.clone.1 | convolution fusion | flops 836757504 | bytes 52742148 | tf_op jit(solution)/shard_map/while/body/eval_jaxpr/vmap(qhe,khe->hqk)/dot_general | solution.py:75
  811.6 21.4 %multiply_convert_fusion.5 = bf16[2,6,512,1024]{3,2,1,0:T(8,128)(2,1)} fusion(f32[2,6,512,1024]{3,2,1,0:T(8,128)} %get-tuple-element.403, f32[2,6,512,1024]{3,2,1,0:T(8,128)} %fusion.128, f32[2,6,512]{2,1,0:T(8,128)S(1)} %get-tuple-element.404, f32[2,6,512]{2,1,0:T(8,128)S(1)} %dynamic-slice_bitcast_fusion.2, pred[2,1024]{1,0:T(4,128)(4,1)S(1)} %iota_compare_fusion.5), kind=kLoop, calls=%fused_computation.15.clone.1 | loop fusion | flops 37748736 | bytes 62965760 | tf_op jit(solution)/shard_map/while/body/eval_jaxpr/vmap()/convert_element_type | solution.py:79
  865.3 12.6 %copy.110 = bf16[2,1024,3,384]{3,0,2,1:T(2,128)(2,1)} copy(bf16[2,1024,3,384]{1,3,0,2:T(8,128)(2,1)} %pad_maximum_fusion.1) | data formatting | bytes 9437184 | tf_op jit(solution)/shard_map/stack | solution.py:144
  884.4 71.0 %all-to-all-done.3 = bf16[2,1024,3,384]{3,0,2,1:T(2,128)(2,1)} async-done(((bf16[2,1024,3,384]{3,0,2,1:T(2,128)(2,1)}), bf16[2,1024,3,384]{3,0,2,1:T(2,128)(2,1)}, u32[]{:S(2)}, u32[]{:S(2)}) %all-to-all-start.3) | async-done | bytes 4718624 | tf_op jit(solution)/shard_map/all_to_all | solution.py:320
  1000.0 27.6 %all-reduce.8 = (bf16[768]{0:T(1024)(128)(2,1)S(1)}, bf16[768]{0:T(1024)(128)(2,1)S(1)}, bf16[768]{0:T(1024)(128)(2,1)S(1)}, bf16[768]{0:T(1024)(128)(2,1)S(1)}, bf16[768]{0:T(1024)(128)(2,1)S(1)}) all-reduce(bf16[768]{0:T(1024)(128)(2,1)S(1)} %dynamic-update-slice.3, ...), channel_id=1, replica_groups=mesh['fsdp'=8,'ctx'=2,'tp'=2] {'fsdp'}, use_global_device_ids=true, to_apply=%add.3 | all-reduce | flops 3840 | bytes 15360
  1042.7 20.3 %reduce-scatter.14.cloned.1.call-done = bf16[96,768]{1,0:T(8,128)(2,1)} async-done(((bf16[768,768]{1,0:T(8,128)(2,1)}), bf16[96,768]{1,0:T(8,128)(2,1)}) %reduce-scatter.14.cloned.1.call-update) | async-done | bytes 147472 | tf_op jit(solution)/shard_map/reduce_scatter | solution.py:153
  1072.9 40.5 %all-reduce.16.cloned.1.call-done = (bf16[96,2304]{0,1:T(8,128)(2,1)}, bf16[96,768]{1,0:T(8,128)(2,1)}) async-done(((bf16[96,2304]{0,1:T(8,128)(2,1)}, bf16[96,768]{1,0:T(8,128)(2,1)}), (bf16[96,2304]{0,1:T(8,128)(2,1)}, bf16[96,768]{1,0:T(8,128)(2,1)})) %all-reduce.16.cloned.1.call-update) | async-done | bytes 589840 | tf_op jit(solution)/shard_map/psum | solution.py:173
  (248 shorter events, 423.8 us)
Async XLA Ops:
  7.2 46.7 %all-gather.8.cloned.1.call-start = ((), (), s32[]{:S(2)}) async-start(), calls=%async_computation.11 | async-start | bytes 3981312 | tf_op jit(solution)/shard_map/all_gather | solution.py:230
  9.8 52.0 %copy-start.14 = (f32[2,512,32]{1,2,0:T(8,128)}, f32[2,512,32]{1,2,0:T(8,128)S(1)}, u32[]{:S(2)}) copy-start(f32[2,512,32]{1,2,0:T(8,128)S(1)} %get-tuple-element.284) | copy-start | bytes 393220
  75.4 59.5 %all-to-all-start = ((bf16[2,512,3,768]{1,0,2,3:T(2,128)(2,1)}), bf16[2,512,3,768]{1,0,2,3:T(2,128)(2,1)}, u32[]{:S(2)}, u32[]{:S(2)}) async-start(bf16[2,512,3,768]{1,0,2,3:T(2,128)(2,1)} %copy.99), calls=%async_computation | async-start | bytes 9437184 | tf_op jit(solution)/shard_map/all_to_all | solution.py:253
  81.2 194.8 %all-gather.10.cloned.1.call-start = ((), (), s32[]{:S(2)}) async-start(), calls=%async_computation.12 | async-start | bytes 1327104 | tf_op jit(solution)/shard_map/all_gather | solution.py:231
  82.0 202.4 %all-gather.14.cloned.1.call-start = ((), (), s32[]{:S(2)}) async-start(), calls=%async_computation.14 | async-start | bytes 2654208 | tf_op jit(solution)/shard_map/all_gather | solution.py:232
  249.3 23.8 %all-to-all-start.1 = ((bf16[2,1024,384]{2,0,1:T(2,128)(2,1)}), bf16[2,1024,384]{2,0,1:T(2,128)(2,1)}, u32[]{:S(2)}, u32[]{:S(2)}) async-start(bf16[2,1024,384]{2,0,1:T(2,128)(2,1)} %copy.104), calls=%async_computation.1 | async-start | bytes 3145728 | tf_op jit(solution)/shard_map/all_to_all | solution.py:255
  253.9 72.3 %all-gather.12.cloned.1.call-start = ((), (), s32[]{:S(2)}) async-start(), calls=%async_computation.13 | async-start | bytes 4718592 | tf_op jit(solution)/shard_map/all_gather | solution.py:264
  283.2 76.2 %all-gather.16.cloned.1.call-start = ((), (), s32[]{:S(2)}) async-start(), calls=%async_computation.15 | async-start | bytes 2654208 | tf_op jit(solution)/shard_map/all_gather | solution.py:233
  283.8 107.9 %all-gather.18.cloned.1.call-start = ((), (), s32[]{:S(2)}) async-start(), calls=%async_computation.16 | async-start | bytes 2654208 | tf_op jit(solution)/shard_map/all_gather | solution.py:234
  284.3 193.2 %reduce-scatter.10.cloned.1.call-start = ((), (), s32[]{:S(2)}) async-start(), calls=%async_computation.17 | async-start | bytes 9437184 | tf_op jit(solution)/shard_map/reduce_scatter | solution.py:276
  401.2 132.0 %all-gather.20.cloned.1.call-start = ((), (), s32[]{:S(2)}) async-start(), calls=%async_computation.18 | async-start | bytes 4718592 | tf_op jit(solution)/shard_map/all_gather | solution.py:281
  401.3 242.6 %copy-start.19 = (f32[768]{0:T(1024)}, f32[768]{0:T(1024)S(1)}, u32[]{:S(2)}) copy-start(f32[768]{0:T(1024)S(1)} %convert_element_type.167) | copy-start | bytes 9220
  481.3 162.5 %copy-start.17 = (f32[2,512]{1,0:T(2,128)}, f32[2,512]{1,0:T(2,128)S(1)}, u32[]{:S(2)}) copy-start(f32[2,512]{1,0:T(2,128)S(1)} %broadcast_multiply_fusion.5) | copy-start | bytes 12292
  483.8 160.0 %copy-start.21 = (f32[2,512]{1,0:T(2,128)}, f32[2,512]{1,0:T(2,128)S(1)}, u32[]{:S(2)}) copy-start(f32[2,512]{1,0:T(2,128)S(1)} %add_rsqrt_fusion) | copy-start | bytes 12292
  488.1 155.8 %reduce-scatter.12.cloned.1.call-start = ((), (), s32[]{:S(2)}) async-start(), calls=%async_computation.19 | async-start | bytes 9437184 | tf_op jit(solution)/shard_map/reduce_scatter | solution.py:307
  566.7 317.0 %reduce-scatter.20.cloned.1.call-start = ((), (), s32[]{:S(2)}) async-start(), calls=%async_computation.23 | async-start | bytes 2654208 | tf_op jit(solution)/shard_map/reduce_scatter | solution.py:190
  576.3 307.4 %reduce-scatter.18.cloned.1.call-start = ((), (), s32[]{:S(2)}) async-start(), calls=%async_computation.22 | async-start | bytes 2654208 | tf_op jit(solution)/shard_map/reduce_scatter | solution.py:187
  660.2 24.2 %all-to-all-start.2 = ((bf16[2,512,768]{1,0,2:T(2,128)(2,1)}), bf16[2,512,768]{1,0,2:T(2,128)(2,1)}, u32[]{:S(2)}, u32[]{:S(2)}) async-start(bf16[2,512,768]{1,0,2:T(2,128)(2,1)} %copy.107), calls=%async_computation.4 | async-start | bytes 3145728 | tf_op jit(solution)/shard_map/all_to_all | solution.py:318
  664.8 218.9 %reduce-scatter.16.cloned.1.call-start = ((), (), s32[]{:S(2)}) async-start(), calls=%async_computation.21 | async-start | bytes 2654208 | tf_op jit(solution)/shard_map/reduce_scatter | solution.py:184
  877.8 77.6 %all-to-all-start.3 = ((bf16[2,1024,3,384]{3,0,2,1:T(2,128)(2,1)}), bf16[2,1024,3,384]{3,0,2,1:T(2,128)(2,1)}, u32[]{:S(2)}, u32[]{:S(2)}) async-start(bf16[2,1024,3,384]{3,0,2,1:T(2,128)(2,1)} %copy.110), calls=%async_computation.5 | async-start | bytes 9437184 | tf_op jit(solution)/shard_map/all_to_all | solution.py:320
  883.6 110.9 %all-reduce.18.cloned.1.call-start = ((), (), s32[]{:S(2)}) async-start(), calls=%async_computation.26 | async-start | bytes 1769472 | tf_op jit(solution)/shard_map/psum | solution.py:198
  884.4 156.3 %reduce-scatter.22.cloned.1.call-start = ((), (), s32[]{:S(2)}) async-start(), calls=%async_computation.24 | async-start | bytes 3981312
  985.8 77.1 %reduce-scatter.14.cloned.1.call-start = ((), (), s32[]{:S(2)}) async-start(), calls=%async_computation.20 | async-start | bytes 1327104 | tf_op jit(solution)/shard_map/reduce_scatter | solution.py:153
  991.7 121.6 %all-reduce.16.cloned.1.call-start = ((), (), s32[]{:S(2)}) async-start(), calls=%async_computation.25 | async-start | bytes 1474560 | tf_op jit(solution)/shard_map/psum | solution.py:173
  (37 other events, 409.5 us)
Sparse Core Ops, SparseCore 0:
  9.7 44.2 all-gather.7
  83.7 22.0 all-gather.9
  107.4 31.2 all-gather.13
  283.3 42.8 all-gather.11
  327.7 31.6 all-gather.15
  360.9 30.7 all-gather.17
  401.3 76.1 reduce-scatter.9
  488.2 44.9 all-gather.19
  566.8 77.0 reduce-scatter.11
  646.0 36.2 reduce-scatter.19
  684.6 35.5 reduce-scatter.17
  722.4 35.3 reduce-scatter.15
  886.9 57.0 all-reduce.17
  985.9 43.3 reduce-scatter.21
  1031.6 31.3 reduce-scatter.13
  1066.9 46.3 all-reduce.15
where the time goes:
time: 1130 us; the launch traced here: 1120 us
  waiting for transfers between devices  507 us (45%)
  matrix products  289 us (26%)
  local copies, waits for them, and re-layouts  124 us (11%)
  other arithmetic  115 us (10%)
  blocking collectives  51 us (5%)
  starting transfers between devices  21.4 us (2%)
  between operations  16.3 us (1%)
    reduce_scatter x1, waiting for transfers between devices, on_device(): lax.psum_scatter(partial_result, 'tp', scatter_dimension=0, tiled=True)  76.3 us
    all_to_all x1, waiting for transfers between devices, on_device(): lax.all_to_all(grad_qkv_heads.astype(jnp.bfloat16), 'ctx', split_axis=1,...  71 us
    reduce_scatter x1, waiting for transfers between devices, on_device(): lax.psum_scatter(feed_partial, 'tp', scatter_dimension=0, tiled=True)  57.7 us
    all_to_all x1, waiting for transfers between devices, on_device(): lax.all_to_all(packed, 'ctx', split_axis=3, concat_axis=1, tiled=True)  52.2 us
    all_gather x1, waiting for transfers between devices, on_device(): lax.all_gather(grad_mix_two.astype(jnp.bfloat16), 'tp', axis=0, tiled=True)  45 us
    all_gather x1, waiting for transfers between devices, on_device(): lax.all_gather(query_key_value_weight, 'fsdp', axis=0, tiled=True)  44.1 us
    convert_element_type x2, other arithmetic, block_backward(): grad_scores = (softmax_out * (grad_probs - row_dot)).astype(jnp.bfloat16)  43.4 us
    unnamed x2, blocking collectives  42 us
  transfers between devices with their start and end apart: 20, of which 13 were waited for; matrix products, arithmetic and copies ran while one was open for 39% of the time, Pallas kernels for 0%

commit v1 on v0

v1 whole, which is shorter than its diff:
```python
import functools

import jax
import jax.numpy as jnp
from jax import lax
from jax.experimental import pallas as pl
from jax.experimental.pallas import tpu as pltpu
from jax.sharding import PartitionSpec as P

HEADS = 12
HEAD_DIM = 64
PAIR = 2 * HEAD_DIM

norm_eps = 1e-05
rope_base = 1000.0
masked_bias = -1000000000.0

bf16 = jnp.bfloat16
f32 = jnp.float32
NN = (((1,), (0,)), ((), ()))
NT = (((1,), (1,)), ((), ()))
VMEM_LIMIT = 60 * 2**20
ANY = pl.BlockSpec(memory_space=pl.ANY)


def dot(left, right, dims=NN):
    return lax.dot_general(left, right, dims, preferred_element_type=f32)


def params():
    return pltpu.CompilerParams(vmem_limit_bytes=VMEM_LIMIT)


def cost(flops, moved, exps=0):
    return pl.CostEstimate(flops=int(flops), bytes_accessed=int(moved), transcendentals=int(exps))


def piece_copies(own, other, spots, full, sems):
    col_blocks, row_blocks, rows, width = own.shape
    copies = []
    for side, source in enumerate((own, other)):
        for row in range(row_blocks):
            for col in range(col_blocks):
                start = pl.multiple_of(spots[side * row_blocks + row], 16)
                left = pl.multiple_of(spots[2 * row_blocks + col], 128)
                copies.append(
                    pltpu.make_async_copy(
                        source.at[col, row],
                        full.at[pl.ds(start, rows), pl.ds(left, width)],
                        sems.at[(side * row_blocks + row) * col_blocks + col],
                    )
                )
    return copies


def piece_count(own):
    return 2 * own.shape[0] * own.shape[1]


def turned(block, cosine, sine):
    lane = lax.broadcasted_iota(jnp.int32, block.shape, 1)
    first = (lane % HEAD_DIM) < HEAD_DIM // 2
    partner = jnp.where(
        first, pltpu.roll(block, PAIR - HEAD_DIM // 2, 1), pltpu.roll(block, HEAD_DIM // 2, 1)
    )
    return block * cosine + partner * sine


def turn_tables(places):
    half_dim = HEAD_DIM // 2
    frequency = rope_base ** (-jnp.arange(half_dim, dtype=f32) * 2.0 / HEAD_DIM)
    angles = places.astype(f32)[:, None] * frequency
    cosine = jnp.cos(angles)
    sine = jnp.sin(angles)
    return jnp.concatenate([cosine] * 4, 1), jnp.concatenate([-sine, sine, -sine, sine], 1)


def project_kernel(spots, tokens, cosine, sine, own, other, q_out, k_out, v_out, weight, sems):
    width = q_out.shape[1]

    @pl.when(pl.program_id(0) == 0)
    def _():
        copies = piece_copies(own, other, spots, weight, sems)
        for copy in copies:
            copy.start()
        for copy in copies:
            copy.wait()

    rows = tokens[...]
    cos_part = cosine[...]
    sin_part = sine[...]
    for part, out in enumerate((q_out, k_out, v_out)):
        raw = dot(rows, weight[:, part * width : (part + 1) * width])
        for pair in range(width // PAIR):
            cols = slice(pair * PAIR, (pair + 1) * PAIR)
            block = raw[:, cols]
            if part < 2:
                block = turned(block, cos_part, sin_part)
            block = block.astype(bf16)
            if part == 0:
                block = block * jnp.asarray(HEAD_DIM**-0.5, bf16)
            out[:, cols] = block


def project(spots, tokens, cosine, sine, own, other, block=256):
    rows, width = tokens.shape
    total = own.shape[0] * own.shape[3]
    row_spec = pl.BlockSpec((block, width), lambda i, *_: (i, 0))
    table = pl.BlockSpec((block, PAIR), lambda i, *_: (i, 0))
    part = total // 3
    out_spec = pl.BlockSpec((block, part), lambda i, *_: (i, 0))
    return pl.pallas_call(
        project_kernel,
        grid_spec=pltpu.PrefetchScalarGridSpec(
            num_scalar_prefetch=1,
            grid=(rows // block,),
            in_specs=[row_spec, table, table, ANY, ANY],
            out_specs=[out_spec] * 3,
            scratch_shapes=[
                pltpu.VMEM((width, total), bf16),
                pltpu.SemaphoreType.DMA((piece_count(own),)),
            ],
        ),
        out_shape=[jax.ShapeDtypeStruct((rows, part), bf16)] * 3,
        compiler_params=params(),
        cost_estimate=cost(2 * rows * width * total, 4 * rows * total + 2 * width * total),
        name="project",
    )(spots, tokens, cosine, sine, own, other)


def lane_ids(shape):
    return lax.broadcasted_iota(jnp.int32, shape, 1)


def key_bias(length, shape):
    return jnp.where(lax.broadcasted_iota(jnp.int32, shape, 0) < length, 0.0, masked_bias).astype(
        bf16
    )


def attend_kernel(length, q_ref, k_ref, v_ref, out_ref, summit_ref):
    lane_q = lane_ids(q_ref.shape)
    lane_k = lane_ids(k_ref.shape)
    bias = key_bias(length[0], k_ref.shape)
    queries = q_ref[...]
    keys = k_ref[...]
    values = v_ref[...]
    one = jnp.ones((), bf16)
    zero = jnp.zeros((), bf16)
    outs = []
    summits = []
    for head in range(2):
        mine_q = (lane_q < HEAD_DIM) if head == 0 else (lane_q >= HEAD_DIM)
        mine_k = (lane_k < HEAD_DIM) if head == 0 else (lane_k >= HEAD_DIM)
        spare = HEAD_DIM * (1 - head)
        query = jnp.where(mine_q, queries, jnp.where(lane_q == spare, one, zero))
        key = jnp.where(mine_k, keys, bias)
        value = jnp.where(mine_k, values, one)
        scores = dot(query, key, NT)
        top = jnp.max(scores, axis=1, keepdims=True)
        summed = dot(jnp.exp(scores - top).astype(bf16), value)
        totals = pltpu.roll(summed, HEAD_DIM, 1)
        outs.append(summed / totals)
        summits.append(top + jnp.log(summed))
    low = lane_q < HEAD_DIM
    out_ref[...] = jnp.where(low, outs[0], outs[1]).astype(bf16)
    summit_ref[0] = jnp.where(low, summits[1], summits[0])


def attend(length, queries, keys, values):
    rows, width = queries.shape
    seq = keys.shape[0]
    pairs = width // PAIR
    q_spec = pl.BlockSpec((rows, PAIR), lambda h, *_: (0, h))
    k_spec = pl.BlockSpec((seq, PAIR), lambda h, *_: (0, h))
    return pl.pallas_call(
        attend_kernel,
        grid_spec=pltpu.PrefetchScalarGridSpec(
            num_scalar_prefetch=1,
            grid=(pairs,),
            in_specs=[q_spec, k_spec, k_spec],
            out_specs=[q_spec, pl.BlockSpec((1, rows, PAIR), lambda h, *_: (h, 0, 0))],
        ),
        out_shape=[
            jax.ShapeDtypeStruct((rows, width), bf16),
            jax.ShapeDtypeStruct((pairs, rows, PAIR), f32),
        ],
        compiler_params=params(),
        cost_estimate=cost(16 * rows * seq * width, 12 * rows * width),
        name="attend",
    )(length, queries, keys, values)


def three_parts(value):
    high = value.astype(bf16)
    rest = value - high.astype(f32)
    middle = rest.astype(bf16)
    return high, middle, (rest - middle.astype(f32)).astype(bf16)


def attend_back_kernel(
    length, q_ref, k_ref, v_ref, out_ref, summit_ref, grad_ref, cos_ref, sin_ref, kcos, ksin, dq_ref, dk_ref, dv_ref
):
    rows = q_ref.shape[0]
    lane_q = lane_ids(q_ref.shape)
    lane_k = lane_ids(k_ref.shape)
    bias = key_bias(length[0], k_ref.shape)
    queries = q_ref[...]
    keys = k_ref[...]
    values = v_ref[...]
    grads = grad_ref[...]
    summit = three_parts(summit_ref[0])
    product = grads.astype(f32) * out_ref[...].astype(f32)
    one = jnp.ones((), bf16)
    zero = jnp.zeros((), bf16)
    grads_t = grads.T
    queries_t = queries.T
    dq, dk, dv = [], [], []
    for head in range(2):
        mine_q = (lane_q < HEAD_DIM) if head == 0 else (lane_q >= HEAD_DIM)
        mine_k = (lane_k < HEAD_DIM) if head == 0 else (lane_k >= HEAD_DIM)
        spare = HEAD_DIM * (1 - head)
        own = slice(HEAD_DIM * head, HEAD_DIM * (head + 1))
        row_dot = jnp.sum(jnp.where(mine_q, product, 0.0), axis=1, keepdims=True)
        row_dot = three_parts(jnp.broadcast_to(row_dot, (rows, PAIR)))

        def beside(main, mine, lane, parts, last):
            extra = jnp.where(lane == spare + 3, last, zero)
            for place in range(3):
                extra = jnp.where(lane == spare + place, parts[place], extra)
            return jnp.where(mine, main, extra)

        minus = (-one, -one, -one)
        query = beside(queries, mine_q, lane_q, summit, one)
        key = beside(keys, mine_k, lane_k, minus, bias)
        grad = beside(grads, mine_q, lane_q, row_dot, zero)
        value = beside(values, mine_k, lane_k, minus, zero)
        probs = jnp.exp(dot(query, key, NT))
        grad_scores = (probs * dot(grad, value, NT)).astype(bf16)
        dv.append(dot(grads_t[own], probs.astype(bf16)))
        dk.append(dot(queries_t[own], grad_scores))
        dq.append(dot(grad_scores, keys))
    grad_query = jnp.where(lane_q < HEAD_DIM, dq[0], dq[1]) * HEAD_DIM**-0.5
    grad_keys = jnp.concatenate(dk, 0).T
    dq_ref[...] = turned(grad_query, cos_ref[...], -sin_ref[...]).astype(bf16)
    dk_ref[...] = turned(grad_keys, kcos[...], -ksin[...]).astype(bf16)
    dv_ref[...] = jnp.concatenate(dv, 0).T.astype(bf16)


def attend_back(length, queries, keys, values, out, summit, grads, cosine, sine, kcos, ksin):
    rows, width = queries.shape
    seq = keys.shape[0]
    pairs = width // PAIR
    q_spec = pl.BlockSpec((rows, PAIR), lambda h, *_: (0, h))
    k_spec = pl.BlockSpec((seq, PAIR), lambda h, *_: (0, h))
    q_table = pl.BlockSpec((rows, PAIR), lambda h, *_: (0, 0))
    k_table = pl.BlockSpec((seq, PAIR), lambda h, *_: (0, 0))
    return pl.pallas_call(
        attend_back_kernel,
        grid_spec=pltpu.PrefetchScalarGridSpec(
            num_scalar_prefetch=1,
            grid=(pairs,),
            in_specs=[
                q_spec,
                k_spec,
                k_spec,
                q_spec,
                pl.BlockSpec((1, rows, PAIR), lambda h, *_: (h, 0, 0)),
                q_spec,
                q_table,
                q_table,
                k_table,
                k_table,
            ],
            out_specs=[q_spec, k_spec, k_spec],
        ),
        out_shape=[jax.ShapeDtypeStruct((count, width), bf16) for count in (rows, seq, seq)],
        compiler_params=params(),
        cost_estimate=cost(40 * rows * seq * width, 16 * rows * width),
        name="attend_back",
    )(length, queries, keys, values, out, summit, grads, cosine, sine, kcos, ksin)


def row_mean(value):
    return jnp.mean(value, axis=-1, keepdims=True)


def normalize(value):
    centered = value - row_mean(value)
    inverse = lax.rsqrt(row_mean(centered * centered) + norm_eps)
    return centered * inverse, inverse


def normalize_back(normed, inverse, gain, upstream):
    scaled = upstream * gain
    return inverse * (scaled - row_mean(scaled) - normed * row_mean(scaled * normed))


def feed_kernel(
    slot_half,
    spots_attn,
    spots_feed,
    tokens,
    context,
    cotangent,
    norms,
    out_own,
    out_other,
    gate_own,
    gate_other,
    up_own,
    up_other,
    down_own,
    down_other,
    mixed,
    hidden,
    dgate,
    dupper,
    feed_t,
    branch_t,
    context_t,
    tokens_t,
    grad_mix_one,
    grad_attn,
    grad_context,
    vectors,
    w_out,
    w_gate,
    w_up,
    w_down,
    gate_pre,
    upper,
    sems,
    chunk=768,
):
    step = pl.program_id(0)
    feed_total = w_gate.shape[1]
    loads = [
        piece_copies(out_own, out_other, spots_attn, w_out, sems.at[0]),
        piece_copies(gate_own, gate_other, spots_feed, w_gate, sems.at[1]),
        piece_copies(up_own, up_other, spots_feed, w_up, sems.at[2]),
        piece_copies(down_own, down_other, spots_feed, w_down, sems.at[3]),
    ]

    @pl.when(step == 0)
    def _():
        for group in loads:
            for copy in group:
                copy.start()
        vectors[...] = jnp.zeros_like(vectors)

    def arrive(group):
        @pl.when(step == 0)
        def _():
            for copy in loads[group]:
                copy.wait()

    gain_one = norms[0:1, :]
    shift_one = norms[1:2, :]
    gain_two = norms[2:3, :]
    shift_two = norms[3:4, :]
    token_rows = tokens[...]
    context_rows = context[...]
    tokens_t[...] = token_rows.T
    context_t[...] = context_rows.T
    arrive(0)
    normed_one, inverse_one = normalize(
        token_rows.astype(f32) + dot(context_rows, w_out[...])
    )
    out_one = normed_one * gain_one + shift_one
    feed_in = out_one.astype(bf16)
    feed_t[...] = feed_in.T
    arrive(1)
    arrive(2)
    arrive(3)
    total = out_one
    for left in range(0, feed_total, chunk):
        cols = slice(left, left + chunk)
        gate = dot(feed_in, w_gate[:, cols])
        up = dot(feed_in, w_up[:, cols])
        gate_pre[:, cols] = gate
        upper[:, cols] = up
        hid = (gate * jax.nn.sigmoid(gate) * up).astype(bf16)
        hidden[:, cols] = hid
        total = total + dot(hid, w_down[:, cols], NT)
    normed_two, inverse_two = normalize(total)
    mixed[0] = (normed_two * gain_two + shift_two).astype(bf16)
    upstream = cotangent[...].astype(f32)
    grad_mix_two = normalize_back(normed_two, inverse_two, gain_two, upstream)
    grad_branch = grad_mix_two.astype(bf16)
    branch_t[...] = grad_branch.T
    grad_out_one = grad_mix_two
    for left in range(0, feed_total, chunk):
        cols = slice(left, left + chunk)
        grad_hidden = dot(grad_branch, w_down[:, cols])
        gate = gate_pre[:, cols]
        sig = jax.nn.sigmoid(gate)
        swish = gate * sig
        grad_gate = (grad_hidden * upper[:, cols] * (sig + swish * (1.0 - sig))).astype(bf16)
        grad_up = (grad_hidden * swish).astype(bf16)
        dgate[:, cols] = grad_gate
        dupper[:, cols] = grad_up
        grad_out_one = (
            grad_out_one + dot(grad_gate, w_gate[:, cols], NT) + dot(grad_up, w_up[:, cols], NT)
        )
    vectors[0:1, :] += jnp.sum(grad_out_one * normed_one, axis=0, keepdims=True)
    vectors[1:2, :] += jnp.sum(grad_out_one, axis=0, keepdims=True)
    vectors[2:3, :] += jnp.sum(upstream * normed_two, axis=0, keepdims=True)
    vectors[3:4, :] += jnp.sum(upstream, axis=0, keepdims=True)
    grad_one = normalize_back(normed_one, inverse_one, gain_one, grad_out_one)
    grad_mix_one[...] = grad_one
    grad_rows = grad_one.astype(bf16)
    grad_attn[...] = grad_rows
    grad_context[...] = dot(grad_rows, w_out[...], NT).astype(bf16)


def feed_forward(
    slot_half, spots_attn, spots_feed, tokens, context, cotangent, norms, out_w, gate_w, up_w, down_w, block=256
):
    rows, width = tokens.shape
    feed_total = gate_w[0].shape[0] * gate_w[0].shape[3]
    half = rows // 2
    halves = half // block
    row_spec = pl.BlockSpec((block, width), lambda i, *_: (i, 0))
    wide_spec = pl.BlockSpec((block, feed_total), lambda i, *_: (i, 0))
    turned_spec = pl.BlockSpec((width, block), lambda i, *_: (0, i))
    mixed_spec = pl.BlockSpec(
        (1, block, width), lambda i, s, *_: ((i // halves + s[0]) % 2, i % halves, 0)
    )
    whole = pl.BlockSpec((8, width), lambda i, *_: (0, 0))
    count = max(piece_count(out_w[0]), piece_count(gate_w[0]))
    return pl.pallas_call(
        feed_kernel,
        grid_spec=pltpu.PrefetchScalarGridSpec(
            num_scalar_prefetch=3,
            grid=(rows // block,),
            in_specs=[row_spec, row_spec, row_spec, whole] + [ANY] * 8,
            out_specs=[mixed_spec]
            + [wide_spec] * 3
            + [turned_spec] * 4
            + [row_spec] * 3
            + [whole],
            scratch_shapes=[
                pltpu.VMEM((width, width), bf16),
                pltpu.VMEM((width, feed_total), bf16),
                pltpu.VMEM((width, feed_total), bf16),
                pltpu.VMEM((width, feed_total), bf16),
                pltpu.VMEM((block, feed_total), f32),
                pltpu.VMEM((block, feed_total), f32),
                pltpu.SemaphoreType.DMA((4, count)),
            ],
        ),
        out_shape=[jax.ShapeDtypeStruct((2, half, width), bf16)]
        + [jax.ShapeDtypeStruct((rows, feed_total), bf16)] * 3
        + [jax.ShapeDtypeStruct((width, rows), bf16)] * 4
        + [
            jax.ShapeDtypeStruct((rows, width), f32),
            jax.ShapeDtypeStruct((rows, width), bf16),
            jax.ShapeDtypeStruct((rows, width), bf16),
            jax.ShapeDtypeStruct((8, width), f32),
        ],
        compiler_params=params(),
        cost_estimate=cost(
            2 * rows * width * (6 * feed_total + 2 * width),
            rows * (6 * feed_total + 20 * width) + 6 * width * feed_total,
        ),
        name="feed_forward",
    )(slot_half, spots_attn, spots_feed, tokens, context, cotangent, norms, *out_w, *gate_w, *up_w, *down_w)


def outer_kernel(spots, left_t, right, keep, send, total):
    row_blocks, rows = keep.shape[1], keep.shape[2]
    total[...] = dot(left_t[...], right[...])
    for side, out in enumerate((keep, send)):
        for row in range(row_blocks):
            start = pl.multiple_of(spots[side * row_blocks + row], 16)
            out[0, row] = total[pl.ds(start, rows), :].astype(bf16)


def outer(spots, left_t, right, col_blocks, row_blocks, chunk=768):
    width, tokens_in = left_t.shape
    columns = right.shape[1]
    rows = width // (2 * row_blocks)
    block = columns // col_blocks
    chunk = min(chunk, block)
    per = block // chunk

    def right_index(i, s):
        return (0, s[2 * row_blocks + i // per] // chunk + i % per)

    out_spec = pl.BlockSpec((1, row_blocks, rows, chunk), lambda i, *_: (i // per, 0, 0, i % per))
    return pl.pallas_call(
        outer_kernel,
        grid_spec=pltpu.PrefetchScalarGridSpec(
            num_scalar_prefetch=1,
            grid=(columns // chunk,),
            in_specs=[
                pl.BlockSpec((width, tokens_in), lambda i, *_: (0, 0)),
                pl.BlockSpec((tokens_in, chunk), right_index),
            ],
            out_specs=[out_spec] * 2,
            scratch_shapes=[pltpu.VMEM((width, chunk), f32)],
        ),
        out_shape=[jax.ShapeDtypeStruct((col_blocks, row_blocks, rows, block), bf16)] * 2,
        compiler_params=params(),
        cost_estimate=cost(
            2 * width * tokens_in * columns, 2 * (width + tokens_in) * columns + 2 * width * tokens_in
        ),
        name="outer",
    )(spots, left_t, right)


def token_kernel(slot_half, spots, grad_q, grad_k, grad_v, grad_one, own, other, keep, send, weight, sems):
    width = grad_one.shape[1]

    @pl.when(pl.program_id(0) == 0)
    def _():
        copies = piece_copies(own, other, spots, weight, sems)
        for copy in copies:
            copy.start()
        for copy in copies:
            copy.wait()

    total = grad_one[...]
    for part, grad in enumerate((grad_q, grad_k, grad_v)):
        total = total + dot(grad[...], weight[:, part * width : (part + 1) * width], NT)
    half = pl.program_id(0) * 2 // pl.num_programs(0)

    @pl.when(half == 0)
    def _():
        send[...] = total.astype(bf16)

    @pl.when(half == 1)
    def _():
        keep[...] = total


def token_gradient(slot_half, spots, grad_raw, grad_one, own, other, block=256):
    rows, width = grad_one.shape
    half = rows // 2
    halves = half // block

    def source(i, s):
        return (i + (1 - s[0]) * halves) % (2 * halves)

    return pl.pallas_call(
        token_kernel,
        grid_spec=pltpu.PrefetchScalarGridSpec(
            num_scalar_prefetch=2,
            grid=(2 * halves,),
            in_specs=[
                pl.BlockSpec((block, width), lambda i, s, *_: (source(i, s), 0)),
                pl.BlockSpec((block, width), lambda i, s, *_: (source(i, s), 0)),
                pl.BlockSpec((block, width), lambda i, s, *_: (source(i, s), 0)),
                pl.BlockSpec((block, width), lambda i, s, *_: (source(i, s), 0)),
                ANY,
                ANY,
            ],
            out_specs=[
                pl.BlockSpec((block, width), lambda i, *_: (jnp.maximum(i - halves, 0), 0)),
                pl.BlockSpec((block, width), lambda i, *_: (jnp.minimum(i, halves - 1), 0)),
            ],
            scratch_shapes=[
                pltpu.VMEM((width, 3 * width), bf16),
                pltpu.SemaphoreType.DMA((piece_count(own),)),
            ],
        ),
        out_shape=[
            jax.ShapeDtypeStruct((half, width), f32),
            jax.ShapeDtypeStruct((half, width), bf16),
        ],
        compiler_params=params(),
        cost_estimate=cost(6 * rows * width * width, 14 * rows * width + 6 * width * width),
        name="token_gradient",
    )(slot_half, spots, *grad_raw, grad_one, own, other)


class Transfers:
    def __init__(self, mesh):
        self.fsdp = mesh.shape["fsdp"]
        self.ctx = mesh.shape["ctx"]
        self.tp = mesh.shape["tp"]
        self.levels = self.fsdp // 2
        place = lax.axis_index("fsdp")
        self.z = place // 2
        self.core = place % 2
        self.x = lax.axis_index("ctx")
        self.y = lax.axis_index("tp")
        self.paired = self.ctx == 2 and self.tp == 2 and self.fsdp % 2 == 0

    def swap_slots(self, value):
        return lax.ppermute(value, "ctx", [(i, i ^ 1) for i in range(self.ctx)])

    def swap(self, value, axis):
        return lax.ppermute(value, axis, [(0, 1), (1, 0)])

    def swap_core(self, value):
        return lax.ppermute(value, "fsdp", [(i, i ^ 1) for i in range(self.fsdp)])

    def shift(self, value, step):
        pairs = [
            (2 * level + core, 2 * ((level + step) % self.levels) + core)
            for level in range(self.levels)
            for core in range(2)
        ]
        return lax.ppermute(value, "fsdp", pairs)

    def row_spots(self, rows, split, sign):
        spots = []
        for side in range(2):
            for part in range(2):
                for step in range(self.levels):
                    level = (self.z + sign * step + self.levels) % self.levels
                    block = 2 * level + jnp.bitwise_xor(self.core, side)
                    spots.append(2 * rows * block + rows * jnp.bitwise_xor(split, part))
        return spots

    def spots(self, rows, split, sign, width=None):
        found = self.row_spots(rows, split, sign)
        if width is None:
            found = found + [jnp.zeros((), jnp.int32)]
        else:
            found = found + [self.y * width, (1 - self.y) * width]
        return jnp.stack(found).astype(jnp.int32)

    def levels_of(self, block):
        return jnp.stack([block] + [self.shift(block, step) for step in range(1, self.levels)])

    def pair(self, block, axis, at):
        return jnp.stack([block, self.swap(block, axis)], at)

    def gather_attention(self, shard):
        half = shard.shape[0] // 2
        block = lax.dynamic_slice_in_dim(shard, self.y * half, half, 0)
        own = self.pair(self.levels_of(block), "tp", 0)
        own = own.reshape((1, 2 * self.levels) + block.shape)
        return own, self.swap_core(own)

    def gather_feed(self, shard, order):
        half = shard.shape[0] // 2
        block = lax.dynamic_slice_in_dim(shard, self.x * half, half, 0)
        own = self.levels_of(block)
        if order == "yx":
            own = self.pair(self.pair(own, "tp", 0), "ctx", 1)
        else:
            own = self.pair(self.pair(own, "ctx", 0), "tp", 0)
        own = own.reshape((2, 2 * self.levels) + block.shape)
        return own, self.swap_core(own)

    def add(self, left, right):
        return (left.astype(f32) + right.astype(f32)).astype(bf16)

    def finish(self, value):
        total = value[0].astype(f32)
        for step in range(1, self.levels):
            total = total + self.shift(value[step], step).astype(f32)
        total = total.astype(bf16)
        other = self.swap(total, "ctx")
        low = jnp.where(self.x == 0, total, other)
        high = jnp.where(self.x == 0, other, total)
        return low, high

    def reduce_feed(self, keep, send, order):
        rows, width = keep.shape[2:]
        value = self.add(keep, self.swap_core(send))
        value = value.reshape(2, 2, self.levels, rows, width)
        if order == "yx":
            value = self.add(value[0], self.swap(value[1], "tp"))
            value = self.add(value[0], self.swap(value[1], "ctx"))
        else:
            value = self.add(value[:, 0], self.swap(value[:, 1], "ctx"))
            value = self.add(value[0], self.swap(value[1], "tp"))
        return jnp.concatenate(self.finish(value), 0).astype(f32)

    def reduce_attention(self, keep, send):
        rows, width = keep.shape[2:]
        value = self.add(keep, self.swap_core(send))
        value = value.reshape(2, self.levels, rows, width)
        value = self.add(value[0], self.swap(value[1], "ctx"))
        value = self.add(value, self.swap(value, "tp"))
        return self.finish(value)

    def vector_pieces(self, vectors, rows, width):
        shard = vectors.shape[1] // self.fsdp
        value = vectors.astype(bf16).reshape(2, 2, self.levels, 2, shard)
        value = jnp.where(self.x == 0, value, value[::-1])
        value = lax.dynamic_slice_in_dim(
            jnp.concatenate([value, value], 2), self.z, self.levels, 2
        )
        value = jnp.where(self.core == 0, value, value[:, :, :, ::-1])
        value = value.transpose(3, 0, 2, 1, 4).reshape(2, 1, 2 * self.levels, 2, shard)
        value = jnp.pad(value, ((0, 0),) * 3 + ((0, rows - 2), (0, width - shard)))
        return value[0], value[1]


def on_device(
    mesh,
    tokens,
    query_key_value_weight,
    output_weight,
    gate_weight,
    up_weight,
    down_weight,
    gain_one,
    shift_one,
    gain_two,
    shift_two,
    lengths,
    positions,
    cotangent,
):
    move = Transfers(mesh)
    shard, model_width = query_key_value_weight.shape[0], tokens.shape[2]
    feed_width = gate_weight.shape[1]
    slot = move.x % 2
    half_rows = tokens.shape[1]

    def to_slot(value):
        keep = jnp.where(slot == 0, value[0], value[1])
        other = move.swap_slots(jnp.where(slot == 0, value[1], value[0]))
        first = jnp.where(slot == 0, keep, other)
        second = jnp.where(slot == 0, other, keep)
        return jnp.concatenate([first, second], 0)

    def from_slot(keep, other):
        return jnp.where(slot == 0, jnp.stack([keep, other]), jnp.stack([other, keep]))

    slot_tokens = to_slot(tokens)
    slot_places = to_slot(positions)
    length = jnp.where(slot == 0, lengths[0:1], lengths[1:2])
    slot_half = slot[None].astype(jnp.int32)
    norms = lax.all_gather(
        jnp.pad(jnp.stack([gain_one, shift_one, gain_two, shift_two]), ((0, 4), (0, 0))),
        "fsdp",
        axis=1,
        tiled=True,
    ).astype(f32)

    down_turned = down_weight.T
    if move.paired:
        half = shard // 2
        attn_in = move.spots(half, move.y, -1)
        attn_out = move.spots(half, move.x, 1)
        feed_in_spots = move.spots(half, move.x, -1, feed_width)
        feed_out_spots = move.spots(half, move.x, 1, feed_width)
        qkv_w = move.gather_attention(query_key_value_weight)
        out_w = move.gather_attention(output_weight)
        gate_w = move.gather_feed(gate_weight, "yx")
        up_w = move.gather_feed(up_weight, "xy")
        down_w = move.gather_feed(down_turned, "yx")
        attn_blocks, feed_cols, feed_blocks = 2 * move.levels, 2, 2 * move.levels
    else:
        middle = model_width // 2
        attn_in = jnp.asarray([0, middle, 0], jnp.int32)
        attn_out = feed_in_spots = feed_out_spots = attn_in

        def whole(value, axes):
            value = lax.all_gather(value, "fsdp", axis=0, tiled=True)
            if axes:
                value = lax.all_gather(value, "tp", axis=1, tiled=True)
            return value[None, None, :middle], value[None, None, middle:]

        qkv_w = whole(query_key_value_weight, False)
        out_w = whole(output_weight, False)
        gate_w = whole(gate_weight, True)
        up_w = whole(up_weight, True)
        down_w = whole(down_turned, True)
        attn_blocks, feed_cols, feed_blocks = 1, 1, 1

    cosine, sine = turn_tables(slot_places)
    queries, key_rows, values = project(attn_in, slot_tokens, cosine, sine, *qkv_w)
    mates = move.ctx // 2
    if mates > 1:
        groups = [[2 * j + s for j in range(mates)] for s in range(2)]

        def gather_rows(value):
            return lax.all_gather(value, "ctx", axis=0, tiled=True, axis_index_groups=groups)

        key_rows = gather_rows(key_rows)
        values = gather_rows(values)
        key_cos, key_sin = jnp.ones((key_rows.shape[0], PAIR), f32), jnp.zeros(
            (key_rows.shape[0], PAIR), f32
        )
    else:
        key_cos, key_sin = cosine, sine
    context, summit = attend(length, queries, key_rows, values)
    slot_cotangent = to_slot(cotangent)
    (
        mixed,
        hidden,
        grad_gate,
        grad_upper,
        feed_t,
        branch_t,
        context_t,
        tokens_t,
        grad_mix_one,
        grad_attn,
        grad_context,
        vectors,
    ) = feed_forward(
        slot_half,
        attn_in,
        feed_in_spots,
        slot_tokens,
        context,
        slot_cotangent,
        norms,
        out_w,
        gate_w,
        up_w,
        down_w,
    )
    mixed_out = from_slot(mixed[0], move.swap_slots(mixed[1]))
    pieces_down = outer(feed_out_spots, branch_t, hidden, feed_cols, feed_blocks)
    pieces_gate = outer(feed_out_spots, feed_t, grad_gate, feed_cols, feed_blocks)
    pieces_up = outer(feed_out_spots, feed_t, grad_upper, feed_cols, feed_blocks)
    pieces_out = outer(attn_out, context_t, grad_attn, 1, attn_blocks)
    grad_raw = attend_back(
        length,
        queries,
        key_rows,
        values,
        context,
        summit,
        grad_context,
        cosine,
        sine,
        key_cos,
        key_sin,
    )
    if mates > 1:
        rows = slot_tokens.shape[0]
        keys_part = lax.psum_scatter(
            jnp.stack(grad_raw[1:]).astype(f32),
            "ctx",
            scatter_dimension=1,
            axis_index_groups=groups,
            tiled=True,
        )
        turned_keys = keys_part[0].reshape(rows, HEADS, 2, HEAD_DIM // 2)
        cos_half = cosine[:, None, : HEAD_DIM // 2]
        sin_half = sine[:, None, HEAD_DIM // 2 : HEAD_DIM]
        first, second = turned_keys[:, :, 0], turned_keys[:, :, 1]
        turned_keys = jnp.stack(
            [first * cos_half + second * sin_half, second * cos_half - first * sin_half], 2
        ).reshape(rows, model_width)
        grad_raw = (grad_raw[0], turned_keys.astype(bf16), keys_part[1].astype(bf16))
    pieces_qkv = [outer(attn_out, tokens_t, grad_raw[part], 1, attn_blocks) for part in range(3)]
    keep_rows, send_rows = token_gradient(slot_half, attn_in, grad_raw, grad_mix_one, *qkv_w)
    grad_tokens = from_slot(keep_rows, move.swap_slots(send_rows).astype(f32))

    if move.paired:
        down_gradient = move.reduce_feed(*pieces_down, "xy").T
        gate_gradient = move.reduce_feed(*pieces_gate, "yx")
        up_gradient = move.reduce_feed(*pieces_up, "xy")
        extra = move.vector_pieces(vectors[:4], 16, model_width)
        low, high = move.reduce_attention(
            *[jnp.concatenate([piece, more], 2) for piece, more in zip(pieces_out, extra)]
        )
        out_gradient = jnp.concatenate([low[:half], high[:half]], 0).astype(f32)
        vector_grads = [
            row[half + place, :shard].astype(f32) for row in (low, high) for place in range(2)
        ]
        qkv_gradient = jnp.concatenate(
            [jnp.concatenate(move.reduce_attention(*pieces), 0) for pieces in pieces_qkv], 1
        ).astype(f32)
    else:

        def scatter(pieces, axes, other):
            value = jnp.concatenate([piece[0, 0] for piece in pieces], 0)
            value = lax.psum(value, axes)
            value = lax.psum_scatter(value, "fsdp", scatter_dimension=0, tiled=True)
            if other:
                value = lax.psum_scatter(value, "tp", scatter_dimension=1, tiled=True)
            return value.astype(f32)

        down_gradient = scatter(pieces_down, "ctx", True).T
        gate_gradient = scatter(pieces_gate, "ctx", True)
        up_gradient = scatter(pieces_up, "ctx", True)
        out_gradient = scatter(pieces_out, ("ctx", "tp"), False)
        qkv_gradient = jnp.concatenate(
            [scatter(pieces, ("ctx", "tp"), False) for pieces in pieces_qkv], 1
        )
        summed = lax.psum(vectors, ("ctx", "tp"))
        summed = lax.psum_scatter(summed, "fsdp", scatter_dimension=1, tiled=True)
        vector_grads = [summed[place] for place in range(4)]
    return (
        mixed_out,
        grad_tokens,
        qkv_gradient,
        out_gradient,
        gate_gradient,
        up_gradient,
        down_gradient,
        *vector_grads,
    )


def solution(mesh):
    in_specs = (
        P(("fsdp", "tp"), "ctx", None),
        P("fsdp", None),
        P("fsdp", None),
        P("fsdp", "tp"),
        P("fsdp", "tp"),
        P("tp", "fsdp"),
        P("fsdp"),
        P("fsdp"),
        P("fsdp"),
        P("fsdp"),
        P(("fsdp", "tp")),
        P(("fsdp", "tp"), "ctx"),
        P(("fsdp", "tp"), "ctx", None),
    )
    out_specs = (
        P(("fsdp", "tp"), "ctx", None),
        P(("fsdp", "tp"), "ctx", None),
        P("fsdp", None),
        P("fsdp", None),
        P("fsdp", "tp"),
        P("fsdp", "tp"),
        P("tp", "fsdp"),
        P("fsdp"),
        P("fsdp"),
        P("fsdp"),
        P("fsdp"),
    )
    return jax.shard_map(
        functools.partial(on_device, mesh),
        mesh=mesh,
        in_specs=in_specs,
        out_specs=out_specs,
        check_vma=False,
    )
```

time: 1130 us -> 592 us (0.52)
  matrix products: 289 us -> 0 us
  waiting for transfers between devices: 507 us -> 227 us
  Pallas kernels: 0 us -> 187 us
  local copies, waits for them, and re-layouts: 124 us -> 19.8 us
  starting transfers between devices: 21.4 us -> 100 us
  other arithmetic: 115 us -> 36.8 us
  blocking collectives: 51 us -> 13.3 us
  between operations: 16.3 us -> 3 us
    dot_general x29 -> x0, matrix products: 289 us -> none  [the longest x4 40.8 us: masked_scores(): jnp.einsum('qhe,khe->hqk', queries, key_rows, preferred_element_type=jnp....]
    ppermute x0 -> x82, waiting for transfers between devices: none -> 227 us  [the longest x29 132 us: swap(): return lax.ppermute(value, axis, [(0, 1), (1, 0)])]
    pallas_call x0 -> x12, Pallas kernels: none -> 187 us  [the longest x1 54.9 us: feed_forward(): pl.pallas_call(feed_kernel, grid_spec=pltpu.PrefetchScalarGridSpec(num_sc...]
    all_gather x7 -> x0, waiting for transfers between devices: 172 us -> none  [the longest x1 45 us: on_device(): lax.all_gather(grad_mix_two.astype(jnp.bfloat16), 'tp', axis=0, tiled=True)]
    reduce_scatter x6 -> x0, waiting for transfers between devices: 154 us -> none  [the longest x1 76.3 us: on_device(): lax.psum_scatter(partial_result, 'tp', scatter_dimension=0, tiled=True)]
    all_to_all x4 -> x0, waiting for transfers between devices: 136 us -> none  [the longest x1 71 us: on_device(): lax.all_to_all(grad_qkv_heads.astype(jnp.bfloat16), 'ctx', split_axis=1,...]
    ppermute x0 -> x82, starting transfers between devices: none -> 100 us  [the longest x36 55.5 us: shift(): return lax.ppermute(value, 'fsdp', pairs)]
    convert_element_type x19 -> x35, other arithmetic: 62.6 us -> 14.1 us  [the longest x21 9.18 us: add(): return (left.astype(f32) + right.astype(f32)).astype(bf16)]
  transfers between devices with their start and end apart: 20 -> 82, of which waited for: 13 -> 33; matrix products, arithmetic and copies ran while one was open for 39% -> 8% of each run, Pallas kernels for 0% -> 14%
where the time goes in v1:
time: 592 us; the launch traced here: 587 us
  waiting for transfers between devices  227 us (38%)
  Pallas kernels  187 us (32%)
  starting transfers between devices  100 us (17%)
  other arithmetic  36.8 us (6%)
  local copies, waits for them, and re-layouts  19.8 us (3%)
  blocking collectives  13.3 us (2%)
    ppermute x29, waiting for transfers between devices, swap(): return lax.ppermute(value, axis, [(0, 1), (1, 0)])  132 us
    ppermute x36, waiting for transfers between devices, shift(): return lax.ppermute(value, 'fsdp', pairs)  57.5 us
    ppermute x36, starting transfers between devices, shift(): return lax.ppermute(value, 'fsdp', pairs)  55.5 us
    pallas_call x1, Pallas kernels, feed_forward(): pl.pallas_call(feed_kernel, grid_spec=pltpu.PrefetchScalarGridSpec(num_sc...  54.9 us
    pallas_call x7, Pallas kernels, outer(): pl.pallas_call(outer_kernel, grid_spec=pltpu.PrefetchScalarGridSpec(num_s...  50.5 us
    pallas_call x1, Pallas kernels, attend_back(): pl.pallas_call(attend_back_kernel, grid_spec=pltpu.PrefetchScalarGridSpec...  37.5 us
    ppermute x5, waiting for transfers between devices, swap_slots(): return lax.ppermute(value, 'ctx', [(i, i ^ 1) for i in range(self.ctx)])  36.8 us
    ppermute x29, starting transfers between devices, swap(): return lax.ppermute(value, axis, [(0, 1), (1, 0)])  36.6 us
  transfers between devices with their start and end apart: 82, of which 33 were waited for; matrix products, arithmetic and copies ran while one was open for 8% of the time, Pallas kernels for 14%

profile of v1, /device:TPU:0, one launch (start us, length us, event | category | flops | bytes accessed | tf_op | source)
XLA Modules:
  0.0 586.7 jit_solution(15449629778408598599)
XLA Ops:
  18.7 13.3 %all-gather = bf16[8,96,8]{1,2,0:T(8,128)(2,1)S(1)} all-gather(bf16[1,96,8]{1,2,0:T(8,128)(2,1)S(1)} %fusion.42), channel_id=1, replica_groups=mesh['fsdp'=8,'ctx'=2,'tp'=2] {'fsdp'}, dimensions={0}, use_global_device_ids=true | all-gather | bytes 13824 | tf_op jit(solution)/shard_map/all_gather | solution.py:732
  53.6 15.1 %collective-permute-done.14 = bf16[48,1536]{1,0:T(8,128)(2,1)S(1)} collective-permute-done((bf16[48,1536]{1,0:T(8,128)(2,1)}, bf16[48,1536]{1,0:T(8,128)(2,1)S(1)}, u32[]{:S(2)}, u32[]{:S(2)}) %collective-permute-start.14) | collective-permute-done | bytes 147488 | tf_op jit(solution)/shard_map/ppermute | solution.py:606
  78.4 10.9 %collective-permute-done.3 = bf16[48,2304]{1,0:T(8,128)(2,1)S(1)} collective-permute-done((bf16[48,2304]{1,0:T(8,128)(2,1)S(1)}, bf16[48,2304]{1,0:T(8,128)(2,1)S(1)}, u32[]{:S(2)}, u32[]{:S(2)}) %collective-permute-start.3) | collective-permute-done | bytes 221216 | tf_op jit(solution)/shard_map/ppermute | solution.py:606
  92.1 6.8 %collective-permute-done.16 = bf16[4,48,1536]{2,1,0:T(8,128)(2,1)S(1)} collective-permute-done((bf16[4,48,1536]{2,1,0:T(8,128)(2,1)S(1)}, bf16[4,48,1536]{2,1,0:T(8,128)(2,1)S(1)}, u32[]{:S(2)}, u32[]{:S(2)}) %collective-permute-start.16) | collective-permute-done | bytes 589856 | tf_op jit(solution)/shard_map/ppermute | solution.py:595
  99.6 11.9 %collective-permute-done.28 = bf16[4,48,1536]{2,1,0:T(8,128)(2,1)S(1)} collective-permute-done((bf16[4,48,1536]{2,1,0:T(8,128)(2,1)S(1)}, bf16[4,48,1536]{2,1,0:T(8,128)(2,1)S(1)}, u32[]{:S(2)}, u32[]{:S(2)}) %collective-permute-start.28) | collective-permute-done | bytes 589856 | tf_op jit(solution)/shard_map/ppermute | solution.py:595
  118.2 12.3 %collective-permute-done.5 = bf16[4,48,2304]{2,1,0:T(8,128)(2,1)S(1)} collective-permute-done((bf16[4,48,2304]{2,1,0:T(8,128)(2,1)S(1)}, bf16[4,48,2304]{2,1,0:T(8,128)(2,1)S(1)}, u32[]{:S(2)}, u32[]{:S(2)}) %collective-permute-start.5) | collective-permute-done | bytes 884768 | tf_op jit(solution)/shard_map/ppermute | solution.py:595
  132.4 23.7 %collective-permute-done.29 = bf16[2,4,48,1536]{3,2,1,0:T(8,128)(2,1)S(1)} collective-permute-done((bf16[2,4,48,1536]{3,2,1,0:T(8,128)(2,1)S(1)}, bf16[2,4,48,1536]{3,2,1,0:T(8,128)(2,1)S(1)}, u32[]{:S(2)}, u32[]{:S(2)}) %collective-permute-start.29) | collective-permute-done | bytes 1179680 | tf_op jit(solution)/shard_map/ppermute | solution.py:595
  161.6 11.3 %collective-permute-done.7 = bf16[512,768]{1,0:T(8,128)(2,1)S(1)} collective-permute-done((bf16[512,768]{1,0:T(8,128)(2,1)S(1)}, bf16[512,768]{1,0:T(8,128)(2,1)S(1)}, u32[]{:S(2)}, u32[]{:S(2)}) %collective-permute-start.7) | collective-permute-done | bytes 786464 | tf_op jit(solution)/shard_map/ppermute | solution.py:592
  174.5 12.9 %collective-permute-done = bf16[512,768]{1,0:T(8,128)(2,1)S(1)} collective-permute-done((bf16[512,768]{1,0:T(8,128)(2,1)S(1)}, bf16[512,768]{1,0:T(8,128)(2,1)S(1)}, u32[]{:S(2)}, u32[]{:S(2)}) %collective-permute-start) | collective-permute-done | bytes 786464 | tf_op jit(solution)/shard_map/ppermute | solution.py:592
  190.1 9.8 %project.1 = (bf16[1024,768]{1,0:T(8,128)(2,1)}, bf16[1024,768]{1,0:T(8,128)(2,1)}, bf16[1024,768]{1,0:T(8,128)(2,1)}) custom-call(s32[17]{0:T(128)} %stack.377.spots.spots_attn, bf16[1024,768]{1,0:T(8,128)(2,1)} %pad_maximum_fusion.4.tokens, f32[1024,128]{1,0:T(8,128)} %get-tuple-element.157.cosine.cos_ref.kcos, ...), custom_call_target="tpu_custom_call" | custom-call | flops 3623878656 | bytes 12976128 | tf_op jit(solution)/shard_map/project/pallas_call | solution.py:112
  199.9 23.5 %attend.1 = (bf16[1024,768]{1,0:T(8,128)(2,1)}, f32[6,1024,128]{2,1,0:T(8,128)}) custom-call(s32[1]{0:T(128)S(6)} %select_n.368.length, bf16[1024,768]{1,0:T(8,128)(2,1)} %get-tuple-element.47.q_ref, bf16[1024,768]{1,0:T(8,128)(2,1)} %get-tuple-element.48.k_ref, bf16[1024,768]{1,0:T(8,128)(2,1)} %get-tuple-element.49.v_ref), custom_call_target="tpu_custom_call" | custom-call | flops 12884901888 | bytes 9437184 | tf_op jit(solution)/shard_map/attend/pallas_call | solution.py:176
  224.2 54.9 %feed_forward.1 = (bf16[2,512,768]{2,1,0:T(8,128)(2,1)}, bf16[1024,3072]{1,0:T(8,128)(2,1)}, bf16[1024,3072]{1,0:T(8,128)(2,1)}, bf16[1024,3072]{1,0:T(8,128)(2,...) custom-call(s32[1]{0:T(128)} %bitcast.slot_half, ...), custom_call_target="tpu_custom_call" | custom-call | flops 31406948352 | bytes 48758784 | tf_op jit(solution)/shard_map/feed_forward/pallas_call | solution.py:432
  279.1 37.5 %attend_back.1 = (bf16[1024,768]{1,0:T(8,128)(2,1)}, bf16[1024,768]{1,0:T(8,128)(2,1)}, bf16[1024,768]{1,0:T(8,128)(2,1)}) custom-call(s32[1]{0:T(128)S(6)} %select_n.368.length, bf16[1024,768]{1,0:T(8,128)(2,1)} %get-tuple-element.47.q_ref, bf16[1024,768]{1,0:T(8,128)(2,1)} %get-tuple-element.48.k_ref, bf16[1024,768]{1,0:T(8,128)(2,1)} %get-tuple-element.49.v_ref, ...), custom_call_target="tpu_custom_call" | custom-call | flops 32212254720 | bytes 12582912 | tf_op jit(solution)/shard_map/attend_back/pallas_call | solution.py:258
  341.8 10.0 %outer.11 = (bf16[2,8,48,1536]{3,2,1,0:T(8,128)(2,1)}, bf16[2,8,48,1536]{3,2,1,0:T(8,128)(2,1)}) custom-call(s32[18]{0:T(128)} %stack.472.spots, bf16[768,1024]{1,0:T(8,128)(2,1)} %get-tuple-element.72.left_t, bf16[1024,3072]{1,0:T(8,128)(2,1)} %get-tuple-element.73.right), custom_call_target="tpu_custom_call" | custom-call | flops 4831838208 | bytes 12582912 | tf_op jit(solution)/shard_map/outer/pallas_call | solution.py:492
  351.8 10.4 %outer.12 = (bf16[2,8,48,1536]{3,2,1,0:T(8,128)(2,1)}, bf16[2,8,48,1536]{3,2,1,0:T(8,128)(2,1)}) custom-call(s32[18]{0:T(128)} %stack.472.spots, bf16[768,1024]{1,0:T(8,128)(2,1)} %get-tuple-element.72.left_t, bf16[1024,3072]{1,0:T(8,128)(2,1)} %get-tuple-element.76.right), custom_call_target="tpu_custom_call" | custom-call | flops 4831838208 | bytes 12582912 | tf_op jit(solution)/shard_map/outer/pallas_call | solution.py:492
  362.2 9.9 %outer.13 = (bf16[2,8,48,1536]{3,2,1,0:T(8,128)(2,1)}, bf16[2,8,48,1536]{3,2,1,0:T(8,128)(2,1)}) custom-call(s32[18]{0:T(128)} %stack.472.spots, bf16[768,1024]{1,0:T(8,128)(2,1)} %get-tuple-element.79.left_t, bf16[1024,3072]{1,0:T(8,128)(2,1)} %get-tuple-element.80.right), custom_call_target="tpu_custom_call" | custom-call | flops 4831838208 | bytes 12582912 | tf_op jit(solution)/shard_map/outer/pallas_call | solution.py:492
  372.1 10.8 %token_gradient.1 = (f32[512,768]{1,0:T(8,128)}, bf16[512,768]{1,0:T(8,128)(2,1)}) custom-call(s32[1]{0:T(128)} %bitcast.slot_half, s32[17]{0:T(128)} %stack.377.spots.spots_attn, bf16[1024,768]{1,0:T(8,128)(2,1)} %get-tuple-element.54.grad_q.right, bf16[1024,768]{1,0:T(8,128)(2,1)} %get-tuple-element.55.grad_k.right, ...), custom_call_target="tpu_custom_call" | custom-call | flops 3623878656 | bytes 14548992 | tf_op jit(solution)/shard_map/token_gradient/pallas_call | solution.py:546
  391.0 12.6 %collective-permute-done.32 = bf16[512,768]{1,0:T(8,128)(2,1)S(1)} collective-permute-done((bf16[512,768]{1,0:T(8,128)(2,1)}, bf16[512,768]{1,0:T(8,128)(2,1)S(1)}, u32[]{:S(2)}, u32[]{:S(2)}) %collective-permute-start.32) | collective-permute-done | bytes 786464 | tf_op jit(solution)/shard_map/ppermute | solution.py:592
  425.3 7.2 %collective-permute-done.42 = bf16[4,48,768]{2,1,0:T(8,128)(2,1)S(1)} collective-permute-done((bf16[4,48,768]{2,1,0:T(8,128)(2,1)S(1)}, bf16[4,48,768]{2,1,0:T(8,128)(2,1)S(1)}, u32[]{:S(2)}, u32[]{:S(2)}) %collective-permute-start.42) | collective-permute-done | bytes 294944 | tf_op jit(solution)/shard_map/ppermute | solution.py:595
  485.4 17.8 %collective-permute-done.62 = bf16[2,4,48,1536]{3,2,1,0:T(8,128)(2,1)S(1)} collective-permute-done((bf16[2,4,48,1536]{3,2,1,0:T(8,128)(2,1)S(1)}, bf16[2,4,48,1536]{3,2,1,0:T(8,128)(2,1)S(1)}, u32[]{:S(2)}, u32[]{:S(2)}) %collective-permute-start.62) | collective-permute-done | bytes 1179680 | tf_op jit(solution)/shard_map/ppermute | solution.py:595
  512.4 23.5 %collective-permute-done.69 = bf16[2,4,48,1536]{3,2,1,0:T(8,128)(2,1)S(1)} collective-permute-done((bf16[2,4,48,1536]{3,2,1,0:T(8,128)(2,1)S(1)}, bf16[2,4,48,1536]{3,2,1,0:T(8,128)(2,1)S(1)}, u32[]{:S(2)}, u32[]{:S(2)}) %collective-permute-start.69) | collective-permute-done | bytes 1179680 | tf_op jit(solution)/shard_map/ppermute | solution.py:595
  537.6 5.8 collective-permute-done.63
  552.3 6.2 %collective-permute-start.79 = (bf16[48,1536]{1,0:T(8,128)(2,1)S(1)}, bf16[48,1536]{1,0:T(8,128)(2,1)S(1)}, u32[]{:S(2)}, u32[]{:S(2)}) collective-permute-start(bf16[48,1536]{1,0:T(8,128)(2,1)S(1)} %get-tuple-element.99), channel_id=1, source_target_pairs={{0,16},{4,20},{8,24},{12,28},{16,0},{20,4},{24,8},{28,12},{1,17},{... | collective-permute-start | bytes 442376 | tf_op jit(solution)/shard_map/ppermute | solution.py:606
  565.1 7.7 %collective-permute-start.72 = (bf16[48,1536]{1,0:T(8,128)(2,1)S(1)}, bf16[48,1536]{1,0:T(8,128)(2,1)S(1)}, u32[]{:S(2)}, u32[]{:S(2)}) collective-permute-start(bf16[48,1536]{1,0:T(8,128)(2,1)S(1)} %get-tuple-element.102), channel_id=1, source_target_pairs={{0,16},{4,20},{8,24},{12,28},{16,0},{20,4},{24,8},{28,12},{1,17},{... | collective-permute-start | bytes 442376 | tf_op jit(solution)/shard_map/ppermute | solution.py:606
  (326 shorter events, 217.8 us)
Async XLA Ops:
  2.3 36.5 %collective-permute-start.9 = (bf16[48,768]{1,0:T(8,128)(2,1)}, bf16[48,768]{1,0:T(8,128)(2,1)}, u32[]{:S(2)}, u32[]{:S(2)}) collective-permute-start(bf16[48,768]{1,0:T(8,128)(2,1)} %constant_dynamic-slice_fusion.2), channel_id=1, source_target_pairs={{0,16},{4,20},{8,24},{12,28},{16,0},{20,4},{24,8},{28,12},{1,17},{... | collective-permute-start | bytes 221192 | tf_op jit(solution)/shard_map/ppermute | solution.py:606
  6.4 38.2 %collective-permute-start.8 = (bf16[48,768]{1,0:T(8,128)(2,1)}, bf16[48,768]{1,0:T(8,128)(2,1)}, u32[]{:S(2)}, u32[]{:S(2)}) collective-permute-start(bf16[48,768]{1,0:T(8,128)(2,1)} %constant_dynamic-slice_fusion.2), channel_id=1, source_target_pairs={{0,8},{4,12},{8,16},{12,20},{16,24},{20,28},{24,0},{28,4},{1,9},{5... | collective-permute-start | bytes 221192 | tf_op jit(solution)/shard_map/ppermute | solution.py:606
  8.0 36.7 %collective-permute-start.10 = (bf16[48,768]{1,0:T(8,128)(2,1)}, bf16[48,768]{1,0:T(8,128)(2,1)}, u32[]{:S(2)}, u32[]{:S(2)}) collective-permute-start(bf16[48,768]{1,0:T(8,128)(2,1)} %constant_dynamic-slice_fusion.2), channel_id=1, source_target_pairs={{0,24},{4,28},{8,0},{12,4},{16,8},{20,12},{24,16},{28,20},{1,25},{... | collective-permute-start | bytes 221192 | tf_op jit(solution)/shard_map/ppermute | solution.py:606
  76.3 39.6 %collective-permute-start.11 = (bf16[4,48,768]{2,1,0:T(8,128)(2,1)S(1)}, bf16[4,48,768]{2,1,0:T(8,128)(2,1)S(1)}, u32[]{:S(2)}, u32[]{:S(2)}) collective-permute-start(bf16[4,48,768]{2,1,0:T(8,128)(2,1)S(1)} %get-tuple-element.133), channel_id=1, source_target_pairs={{0,1},{1,0},{2,3},{3,2},{4,5},{5,4},{6,7},{7,6},{8,9},{9,8},{10,11... | collective-permute-start | bytes 884744 | tf_op jit(solution)/shard_map/ppermute | solution.py:595
  91.5 39.0 %collective-permute-start.5 = (bf16[4,48,2304]{2,1,0:T(8,128)(2,1)S(1)}, bf16[4,48,2304]{2,1,0:T(8,128)(2,1)S(1)}, u32[]{:S(2)}, u32[]{:S(2)}) collective-permute-start(bf16[4,48,2304]{2,1,0:T(8,128)(2,1)S(1)} %get-tuple-element.96), channel_id=1, source_target_pairs={{0,1},{1,0},{2,3},{3,2},{4,5},{5,4},{6,7},{7,6},{8,9},{9,8},{10,11... | collective-permute-start | bytes 2654216 | tf_op jit(solution)/shard_map/ppermute | solution.py:595
  111.7 44.4 %collective-permute-start.29 = (bf16[2,4,48,1536]{3,2,1,0:T(8,128)(2,1)S(1)}, bf16[2,4,48,1536]{3,2,1,0:T(8,128)(2,1)S(1)}, u32[]{:S(2)}, u32[]{:S(2)}) collective-permute-start(bf16[2,4,48,1536]{3,2,1,0:T(8,128)(2,1)S(1)} %get-tuple-element.92), channel_id=1, source_target_pairs={{0,2},{2,0},{1,3},{3,1},{4,6},{6,4},{5,7},{7,5},{8,10},{10,8},{9,1... | collective-permute-start | bytes 3538952 | tf_op jit(solution)/shard_map/ppermute | solution.py:595
  112.4 47.1 %collective-permute-start.23 = (bf16[2,4,48,1536]{3,2,1,0:T(8,128)(2,1)S(1)}, bf16[2,4,48,1536]{3,2,1,0:T(8,128)(2,1)S(1)}, u32[]{:S(2)}, u32[]{:S(2)}) collective-permute-start(bf16[2,4,48,1536]{3,2,1,0:T(8,128)(2,1)S(1)} %pad_maximum_fusion.7), channel_id=1, source_target_pairs={{0,1},{1,0},{2,3},{3,2},{4,5},{5,4},{6,7},{7,6},{8,9},{9,8},{10,11... | collective-permute-start | bytes 3538952 | tf_op jit(solution)/shard_map/ppermute | solution.py:595
  115.8 57.1 %collective-permute-start.7 = (bf16[512,768]{1,0:T(8,128)(2,1)S(1)}, bf16[512,768]{1,0:T(8,128)(2,1)S(1)}, u32[]{:S(2)}, u32[]{:S(2)}) collective-permute-start(bf16[512,768]{1,0:T(8,128)(2,1)S(1)} %copy-done.10), channel_id=1, source_target_pairs={{0,2},{2,0},{1,3},{3,1},{4,6},{6,4},{5,7},{7,5},{8,10},{10,8},{9,1... | collective-permute-start | bytes 2359304 | tf_op jit(solution)/shard_map/ppermute | solution.py:592
  130.5 57.0 %collective-permute-start = (bf16[512,768]{1,0:T(8,128)(2,1)S(1)}, bf16[512,768]{1,0:T(8,128)(2,1)S(1)}, u32[]{:S(2)}, u32[]{:S(2)}) collective-permute-start(bf16[512,768]{1,0:T(8,128)(2,1)S(1)} %select_bitcast_fusion.1), channel_id=1, source_target_pairs={{0,2},{2,0},{1,3},{3,1},{4,6},{6,4},{5,7},{7,5},{8,10},{10,8},{9,1... | collective-permute-start | bytes 2359304 | tf_op jit(solution)/shard_map/ppermute | solution.py:592
  131.2 57.6 %collective-permute-start.6 = (bf16[1,8,48,2304]{3,2,1,0:T(8,128)(2,1)S(1)}, bf16[1,8,48,2304]{3,2,1,0:T(8,128)(2,1)S(1)}, u32[]{:S(2)}, u32[]{:S(2)}) collective-permute-start(bf16[1,8,48,2304]{3,2,1,0:T(8,128)(2,1)S(1)} %bitcast.321), channel_id=1, source_target_pairs={{0,4},{4,0},{8,12},{12,8},{16,20},{20,16},{24,28},{28,24},{1,5},{5... | collective-permute-start | bytes 5308424 | tf_op jit(solution)/shard_map/ppermute | solution.py:598
  161.1 62.3 %collective-permute-start.24 = (bf16[2,8,48,1536]{3,2,1,0:T(8,128)(2,1)}, bf16[2,8,48,1536]{3,2,1,0:T(8,128)(2,1)}, u32[]{:S(2)}, u32[]{:S(2)}) collective-permute-start(bf16[2,8,48,1536]{3,2,1,0:T(8,128)(2,1)} %pad_maximum_fusion.1.up_own), channel_id=1, source_target_pairs={{0,4},{4,0},{8,12},{12,8},{16,20},{20,16},{24,28},{28,24},{1,5},{5... | collective-permute-start | bytes 7077896 | tf_op jit(solution)/shard_map/ppermute | solution.py:598
  161.1 62.3 %collective-permute-start.30 = (bf16[2,8,48,1536]{3,2,1,0:T(8,128)(2,1)}, bf16[2,8,48,1536]{3,2,1,0:T(8,128)(2,1)}, u32[]{:S(2)}, u32[]{:S(2)}) collective-permute-start(bf16[2,8,48,1536]{3,2,1,0:T(8,128)(2,1)} %bitcast.89.down_own), channel_id=1, source_target_pairs={{0,4},{4,0},{8,12},{12,8},{16,20},{20,16},{24,28},{28,24},{1,5},{5... | collective-permute-start | bytes 7077896 | tf_op jit(solution)/shard_map/ppermute | solution.py:598
  173.0 50.5 %collective-permute-start.18 = (bf16[2,8,48,1536]{3,2,1,0:T(8,128)(2,1)}, bf16[2,8,48,1536]{3,2,1,0:T(8,128)(2,1)}, u32[]{:S(2)}, u32[]{:S(2)}) collective-permute-start(bf16[2,8,48,1536]{3,2,1,0:T(8,128)(2,1)} %bitcast.71.gate_own), channel_id=1, source_target_pairs={{0,4},{4,0},{8,12},{12,8},{16,20},{20,16},{24,28},{28,24},{1,5},{5... | collective-permute-start | bytes 7077896 | tf_op jit(solution)/shard_map/ppermute | solution.py:598
  187.4 36.0 %collective-permute-start.12 = (bf16[1,8,48,768]{3,2,1,0:T(8,128)(2,1)}, bf16[1,8,48,768]{3,2,1,0:T(8,128)(2,1)S(1)}, u32[]{:S(2)}, u32[]{:S(2)}) collective-permute-start(bf16[1,8,48,768]{3,2,1,0:T(8,128)(2,1)} %bitcast.62.out_own), channel_id=1, source_target_pairs={{0,4},{4,0},{8,12},{12,8},{16,20},{20,16},{24,28},{28,24},{1,5},{5... | collective-permute-start | bytes 1769480 | tf_op jit(solution)/shard_map/ppermute | solution.py:598
  333.8 49.1 %collective-permute-start.47 = (bf16[1,8,48,768]{3,2,1,0:T(8,128)(2,1)}, bf16[1,8,48,768]{3,2,1,0:T(8,128)(2,1)}, u32[]{:S(2)}, u32[]{:S(2)}) collective-permute-start(bf16[1,8,48,768]{3,2,1,0:T(8,128)(2,1)} %get-tuple-element.66), channel_id=1, source_target_pairs={{0,4},{4,0},{8,12},{12,8},{16,20},{20,16},{24,28},{28,24},{1,5},{5... | collective-permute-start | bytes 1769480 | tf_op jit(solution)/shard_map/ppermute | solution.py:598
  334.4 51.5 %collective-permute-start.40 = (bf16[1,8,48,768]{3,2,1,0:T(8,128)(2,1)}, bf16[1,8,48,768]{3,2,1,0:T(8,128)(2,1)}, u32[]{:S(2)}, u32[]{:S(2)}) collective-permute-start(bf16[1,8,48,768]{3,2,1,0:T(8,128)(2,1)} %get-tuple-element.64), channel_id=1, source_target_pairs={{0,4},{4,0},{8,12},{12,8},{16,20},{20,16},{24,28},{28,24},{1,5},{5... | collective-permute-start | bytes 1769480 | tf_op jit(solution)/shard_map/ppermute | solution.py:598
  334.4 52.8 %collective-permute-start.33 = (bf16[1,8,48,768]{3,2,1,0:T(8,128)(2,1)}, bf16[1,8,48,768]{3,2,1,0:T(8,128)(2,1)}, u32[]{:S(2)}, u32[]{:S(2)}) collective-permute-start(bf16[1,8,48,768]{3,2,1,0:T(8,128)(2,1)} %get-tuple-element.62), channel_id=1, source_target_pairs={{0,4},{4,0},{8,12},{12,8},{16,20},{20,16},{24,28},{28,24},{1,5},{5... | collective-permute-start | bytes 1769480 | tf_op jit(solution)/shard_map/ppermute | solution.py:598
  341.1 48.0 %collective-permute-start.54 = (bf16[1,8,64,768]{3,2,1,0:T(8,128)(2,1)S(1)}, bf16[1,8,64,768]{3,2,1,0:T(8,128)(2,1)}, u32[]{:S(2)}, u32[]{:S(2)}) collective-permute-start(bf16[1,8,64,768]{3,2,1,0:T(8,128)(2,1)S(1)} %pad_maximum_fusion.10), channel_id=1, source_target_pairs={{0,4},{4,0},{8,12},{12,8},{16,20},{20,16},{24,28},{28,24},{1,5},{5... | collective-permute-start | bytes 2359304 | tf_op jit(solution)/shard_map/ppermute | solution.py:598
  341.2 65.9 %collective-permute-start.31 = (bf16[512,768]{1,0:T(8,128)(2,1)S(1)}, bf16[512,768]{1,0:T(8,128)(2,1)}, u32[]{:S(2)}, u32[]{:S(2)}) collective-permute-start(bf16[512,768]{1,0:T(8,128)(2,1)S(1)} %copy-done.11), channel_id=1, source_target_pairs={{0,2},{2,0},{1,3},{3,1},{4,6},{6,4},{5,7},{7,5},{8,10},{10,8},{9,1... | collective-permute-start | bytes 2359304 | tf_op jit(solution)/shard_map/ppermute | solution.py:592
  385.9 92.1 %collective-permute-start.61 = (bf16[2,8,48,1536]{3,2,1,0:T(8,128)(2,1)}, bf16[2,8,48,1536]{3,2,1,0:T(8,128)(2,1)S(1)}, u32[]{:S(2)}, u32[]{:S(2)}) collective-permute-start(bf16[2,8,48,1536]{3,2,1,0:T(8,128)(2,1)} %get-tuple-element.75), channel_id=1, source_target_pairs={{0,4},{4,0},{8,12},{12,8},{16,20},{20,16},{24,28},{28,24},{1,5},{5... | collective-permute-start | bytes 7077896 | tf_op jit(solution)/shard_map/ppermute | solution.py:598
  387.3 93.5 %collective-permute-start.75 = (bf16[2,8,48,1536]{3,2,1,0:T(8,128)(2,1)S(1)}, bf16[2,8,48,1536]{3,2,1,0:T(8,128)(2,1)S(1)}, u32[]{:S(2)}, u32[]{:S(2)}) collective-permute-start(bf16[2,8,48,1536]{3,2,1,0:T(8,128)(2,1)S(1)} %copy-done.25), channel_id=1, source_target_pairs={{0,4},{4,0},{8,12},{12,8},{16,20},{20,16},{24,28},{28,24},{1,5},{5... | collective-permute-start | bytes 7077896 | tf_op jit(solution)/shard_map/ppermute | solution.py:598
  483.9 51.9 %collective-permute-start.69 = (bf16[2,4,48,1536]{3,2,1,0:T(8,128)(2,1)S(1)}, bf16[2,4,48,1536]{3,2,1,0:T(8,128)(2,1)S(1)}, u32[]{:S(2)}, u32[]{:S(2)}) collective-permute-start(bf16[2,4,48,1536]{3,2,1,0:T(8,128)(2,1)S(1)} %slice_bitcast_fusion.2), channel_id=1, source_target_pairs={{0,2},{2,0},{1,3},{3,1},{4,6},{6,4},{5,7},{7,5},{8,10},{10,8},{9,1... | collective-permute-start | bytes 3538952 | tf_op jit(solution)/shard_map/ppermute | solution.py:595
  503.5 39.9 %collective-permute-start.63 = (bf16[4,48,1536]{2,1,0:T(8,128)(2,1)S(1)}, bf16[4,48,1536]{2,1,0:T(8,128)(2,1)S(1)}, u32[]{:S(2)}, u32[]{:S(2)}) collective-permute-start(bf16[4,48,1536]{2,1,0:T(8,128)(2,1)S(1)} %slice_bitcast_fusion.9), channel_id=1, source_target_pairs={{0,2},{2,0},{1,3},{3,1},{4,6},{6,4},{5,7},{7,5},{8,10},{10,8},{9,1... | collective-permute-start | bytes 1769480 | tf_op jit(solution)/shard_map/ppermute | solution.py:595
  510.9 36.6 %collective-permute-start.77 = (bf16[4,48,1536]{2,1,0:T(8,128)(2,1)S(1)}, bf16[4,48,1536]{2,1,0:T(8,128)(2,1)S(1)}, u32[]{:S(2)}, u32[]{:S(2)}) collective-permute-start(bf16[4,48,1536]{2,1,0:T(8,128)(2,1)S(1)} %slice_bitcast_fusion.5), channel_id=1, source_target_pairs={{0,1},{1,0},{2,3},{3,2},{4,5},{5,4},{6,7},{7,6},{8,9},{9,8},{10,11... | collective-permute-start | bytes 1769480 | tf_op jit(solution)/shard_map/ppermute | solution.py:595
  (86 other events, 1131.1 us)
